TPU v7x, 256 devices: a whole 4x4x8 slice. The times are simulated.
256 devices in a mesh: row: 8 (over x_lo, y), col: 32 (over z, x_hi, core).
Axes of the slice: x: 4 (x_hi: 2, x_lo: 2; x = x_hi * 2 + x_lo), y: 4, z: 8, core: 2. Of those that a mesh axis runs over, the one named last changes fastest.
Arguments:
- weight: bfloat16 [4096, 8192], P('row', 'col'), may hold values from -6 to 6
- grad: bfloat16 [4096, 8192], P('row', 'col'), may hold values from -6 to 6
- moment_first: float32 [4096, 8192], P('row', 'col'), may hold values from -2 to 2
- moment_second: float32 [4096, 8192], P('row', 'col'), may hold values from 0.05 to 5
- basis_left: bfloat16 [4096, 4096], P('col', 'row'), may hold values from -0.13 to 1.13
- basis_right: bfloat16 [8192, 8192], P('col', 'row'), may hold values from -0.13 to 1.13
Outputs:
- new_weight: bfloat16 [4096, 8192], P('row', 'col')
- update: bfloat16 [4096, 8192], P('row', 'col')
- first_new: float32 [4096, 8192], P('row', 'col')
- second_new: float32 [4096, 8192], P('row', 'col')
All inputs are finite; a program needn't handle non-finite values.
Results may differ from a plain program's by a relative error of at most 0.018.
Values may be sent and summed in bfloat16 or wider, within the bound.
A program may use at most 128 MiB of HBM per device.

v0:
```python
import jax
import jax.numpy as jnp
from jax import lax
from jax.sharding import PartitionSpec as P

beta_first = 0.9
beta_second = 0.95
correct_first = 1.0 - 0.9**10
correct_second = 1.0 - 0.95**10
epsilon = 1e-08
learn_rate = 0.001
decay_rate = 0.1


def on_device(weight, grad, moment_first, moment_second, basis_left, basis_right):
    left_cols = lax.all_gather(basis_left, "col", axis=0, tiled=True)
    right_rows = lax.all_gather(basis_right, "row", axis=1, tiled=True)
    right_sum = lax.psum_scatter(
        lax.dot_general(
            right_rows, grad, (((0,), (1,)), ((), ())), preferred_element_type=jnp.float32
        ).astype(jnp.bfloat16),
        "col",
        scatter_dimension=0,
        tiled=True,
    )
    half_cols = lax.all_gather(right_sum, "row", axis=1, tiled=True)
    rotated = lax.dot_general(
        left_cols, half_cols, (((0,), (1,)), ((), ())), preferred_element_type=jnp.float32
    )
    first_new = beta_first * moment_first + (1.0 - beta_first) * rotated
    second_new = beta_second * moment_second + (1.0 - beta_second) * rotated * rotated
    step_rotated = (
        first_new / correct_first / (jnp.sqrt(second_new / correct_second) + epsilon)
    ).astype(jnp.bfloat16)
    left_back = lax.psum_scatter(
        jnp.dot(left_cols, step_rotated, preferred_element_type=jnp.float32).astype(jnp.bfloat16),
        "row",
        scatter_dimension=0,
        tiled=True,
    )
    direction = lax.dot_general(
        lax.all_gather(left_back, "col", axis=1, tiled=True),
        right_rows,
        (((1,), (1,)), ((), ())),
        preferred_element_type=jnp.float32,
    )
    update = direction.astype(jnp.bfloat16)
    weight_wide = weight.astype(jnp.float32)
    new_weight = (weight_wide - learn_rate * (direction + decay_rate * weight_wide)).astype(
        jnp.bfloat16
    )
    return (new_weight, update, first_new, second_new)


def solution(mesh):
    in_specs = (
        P("row", "col"),
        P("row", "col"),
        P("row", "col"),
        P("row", "col"),
        P("col", "row"),
        P("col", "row"),
    )
    out_specs = (P("row", "col"), P("row", "col"), P("row", "col"), P("row", "col"))
    return jax.shard_map(
        on_device, mesh=mesh, in_specs=in_specs, out_specs=out_specs, check_vma=False
    )
```

profile of v0, /device:TPU:1, one launch (start us, length us, event | category | flops | bytes accessed | tf_op | source)
XLA Modules:
  0.0 530.5 jit_solution(5786870800225600729)
XLA Ops:
  7.2 0.0 copy-start
  7.2 0.0 all-gather.5.cloned.1.call-start
  7.2 0.7 all-gather.5.cloned.1.call-update
  7.9 0.0 reduce-scatter.3.cloned.1.call-start
  8.0 60.8 %all-gather.5.cloned.1.call-done = bf16[256,8192]{1,0:T(8,128)(2,1)} async-done(((bf16[256,1024]{1,0:T(8,128)(2,1)}), bf16[256,8192]{1,0:T(8,128)(2,1)}) %all-gather.5.cloned.1.call-update) | async-done | bytes 4194320 | tf_op jit(solution)/shard_map/all_gather | solution.py:17
  68.8 7.8 %convolution_convert_fusion = bf16[8192,512]{1,0:T(8,128)(2,1)} fusion(bf16[256,8192]{1,0:T(8,128)(2,1)} %all-gather.5.cloned.1.call-done, bf16[512,256]{1,0:T(8,128)(2,1)S(1)} %copy-done), kind=kOutput, calls=%fused_computation | convolution fusion | flops 2151677952 | bytes 12845056 | tf_op jit(solution)/shard_map/dot_general | solution.py:19
  76.6 0.0 reduce-scatter.3.cloned.1.call-update
  76.7 0.0 all-gather.9.cloned.1.call-start
  76.7 0.7 all-gather.9.cloned.1.call-update
  77.4 0.0 all-gather.7.cloned.1.call-start
  77.4 147.8 %reduce-scatter.3.cloned.1.call-done = bf16[256,512]{1,0:T(8,128)(2,1)} async-done(((bf16[8192,512]{1,0:T(8,128)(2,1)}), bf16[256,512]{1,0:T(8,128)(2,1)}) %reduce-scatter.3.cloned.1.call-update) | async-done | bytes 262160 | tf_op jit(solution)/shard_map/reduce_scatter | solution.py:18
  225.3 0.0 all-gather.7.cloned.1.call-update
  225.3 0.0 reduce-scatter.5.cloned.1.call-start
  225.4 0.2 copy.11
  225.6 0.2 copy.12
  225.8 92.1 %all-gather.9.cloned.1.call-done = bf16[4096,512]{1,0:T(8,128)(2,1)} async-done(((bf16[128,512]{1,0:T(8,128)(2,1)}), bf16[4096,512]{1,0:T(8,128)(2,1)}) %all-gather.9.cloned.1.call-update) | async-done | bytes 4194320 | tf_op jit(solution)/shard_map/all_gather | solution.py:16
  317.9 36.8 %all-gather.7.cloned.1.call-done = bf16[256,4096]{1,0:T(8,128)(2,1)} async-done(((bf16[256,512]{1,0:T(8,128)(2,1)}), bf16[256,4096]{1,0:T(8,128)(2,1)}) %all-gather.7.cloned.1.call-update) | async-done | bytes 2097168 | tf_op jit(solution)/shard_map/all_gather | solution.py:26
  354.7 4.3 multiply_add_fusion
  359.0 0.0 copy-start.4
  359.0 2.8 fusion
  361.8 0.0 reduce-scatter.5.cloned.1.call-update
  361.8 0.0 all-gather.11.cloned.1.call-start
  361.8 44.8 %reduce-scatter.5.cloned.1.call-done = bf16[512,256]{0,1:T(8,128)(2,1)} async-done(((bf16[4096,256]{0,1:T(8,128)(2,1)}), bf16[512,256]{0,1:T(8,128)(2,1)}) %reduce-scatter.5.cloned.1.call-update) | async-done | bytes 262160 | tf_op jit(solution)/shard_map/reduce_scatter | solution.py:35
  406.6 0.0 all-gather.11.cloned.1.call-update
  406.7 0.1 copy.10
  406.8 1.0 copy.15
  407.8 1.0 copy.16
  408.8 106.1 %all-gather.11.cloned.1.call-done = bf16[512,8192]{0,1:T(8,128)(2,1)} async-done(((bf16[512,256]{0,1:T(8,128)(2,1)}), bf16[512,8192]{0,1:T(8,128)(2,1)}) %all-gather.11.cloned.1.call-update) | async-done | bytes 8388624 | tf_op jit(solution)/shard_map/all_gather | solution.py:42
  514.9 7.7 %fusion.11 = (bf16[512,256]{1,0:T(8,128)(2,1)}, f32[512,256]{1,0:T(8,128)S(1)}) fusion(bf16[512,8192]{0,1:T(8,128)(2,1)} %all-gather.11.cloned.1.call-done, bf16[256,8192]{1,0:T(8,128)(2,1)} %all-gather.5.cloned.1.call-done), kind=kOutput, calls=%fused_computation.19 | convolution fusion | flops 2147614720 | bytes 13369344 | tf_op jit(solution)/shard_map/dot_general | solution.py:41
  522.5 0.2 copy.13
  522.7 0.1 fusion.3
  522.9 0.8 copy.14
  (8 shorter events, 0.0 us)
Async XLA Ops:
  7.2 61.6 %copy-start = (bf16[512,256]{1,0:T(8,128)(2,1)S(1)}, bf16[512,256]{1,0:T(8,128)(2,1)}, u32[]{:S(2)}) copy-start(bf16[512,256]{1,0:T(8,128)(2,1)} %param.7) | copy-start | bytes 786436
  7.2 61.6 %all-gather.5.cloned.1.call-start = ((), (), s32[]{:S(2)}) async-start(), calls=%async_computation.2 | async-start | bytes 4718592 | tf_op jit(solution)/shard_map/all_gather | solution.py:17
  7.9 217.4 %reduce-scatter.3.cloned.1.call-start = ((), (), s32[]{:S(2)}) async-start(), calls=%async_computation.3 | async-start | bytes 8650752 | tf_op jit(solution)/shard_map/reduce_scatter | solution.py:18
  76.6 148.7 %copy-start.2 = (f32[512,256]{1,0:T(8,128)S(1)}, f32[512,256]{1,0:T(8,128)}, u32[]{:S(2)}) copy-start(f32[512,256]{1,0:T(8,128)} %param.8) | copy-start | bytes 1572868
  76.6 148.9 %copy-start.3 = (f32[512,256]{1,0:T(8,128)S(1)}, f32[512,256]{1,0:T(8,128)}, u32[]{:S(2)}) copy-start(f32[512,256]{1,0:T(8,128)} %param.9) | copy-start | bytes 1572868
  76.7 241.2 %all-gather.9.cloned.1.call-start = ((), (), s32[]{:S(2)}) async-start(), calls=%async_computation.5 | async-start | bytes 4325376 | tf_op jit(solution)/shard_map/all_gather | solution.py:16
  77.4 277.3 %all-gather.7.cloned.1.call-start = ((), (), s32[]{:S(2)}) async-start(), calls=%async_computation.4 | async-start | bytes 2359296 | tf_op jit(solution)/shard_map/all_gather | solution.py:26
  225.3 181.3 %reduce-scatter.5.cloned.1.call-start = ((), (), s32[]{:S(2)}) async-start(), calls=%async_computation.6 | async-start | bytes 2359296 | tf_op jit(solution)/shard_map/reduce_scatter | solution.py:35
  354.7 4.3 copy-start.1
  359.0 47.7 %copy-start.4 = (bf16[512,256]{1,0:T(8,128)(2,1)S(1)}, bf16[512,256]{1,0:T(8,128)(2,1)}, u32[]{:S(2)}) copy-start(bf16[512,256]{1,0:T(8,128)(2,1)} %param.6) | copy-start | bytes 786436
  361.8 153.1 %all-gather.11.cloned.1.call-start = ((), (), s32[]{:S(2)}) async-start(), calls=%async_computation.7 | async-start | bytes 8650752 | tf_op jit(solution)/shard_map/all_gather | solution.py:42
Sparse Core Ops, SparseCore 0:
  9.8 58.9 all-gather.4
  76.8 148.4 reduce-scatter.2
  228.1 89.7 all-gather.8
  319.5 35.0 all-gather.6
  361.9 44.6 reduce-scatter.4
  409.3 105.5 all-gather.10
where the time goes:
time: 531 us
  waiting for transfers between devices  490 us (92%)
  matrix products  22.6 us (4%)
  between operations  14.2 us (3%)
    reduce_scatter x1, waiting for transfers between devices, on_device(): lax.psum_scatter(lax.dot_general(right_rows, grad, (((0,), (1,)), ((), ()...  148 us
    all_gather x1, waiting for transfers between devices, on_device(): lax.all_gather(left_back, 'col', axis=1, tiled=True)  106 us
    all_gather x1, waiting for transfers between devices, on_device(): left_cols = lax.all_gather(basis_left, 'col', axis=0, tiled=True)  92.1 us
    all_gather x1, waiting for transfers between devices, on_device(): right_rows = lax.all_gather(basis_right, 'row', axis=1, tiled=True)  60.8 us
    reduce_scatter x1, waiting for transfers between devices, on_device(): lax.psum_scatter(jnp.dot(left_cols, step_rotated, preferred_element_type=...  44.8 us
    all_gather x1, waiting for transfers between devices, on_device(): half_cols = lax.all_gather(right_sum, 'row', axis=1, tiled=True)  36.8 us
  transfers between devices with their start and end apart: 6, of which 6 were waited for; matrix products, arithmetic and copies ran while one was open for 0% of the time, Pallas kernels for 0%

commit v1 on v0

v1 whole, which is shorter than its diff:
```python
import jax
import jax.numpy as jnp
from jax import lax
from jax.experimental import pallas as pl
from jax.experimental.pallas import tpu as pltpu
from jax.sharding import PartitionSpec as P

beta_first = 0.9
beta_second = 0.95
correct_first = 1.0 - 0.9**10
correct_second = 1.0 - 0.95**10
epsilon = 1e-08
learn_rate = 0.001
decay_rate = 0.1

ROWS = 512
COLS = 256
HALF = 128
N_MSG = 160

f32 = jnp.float32
bf16 = jnp.bfloat16


def kernel(
    weight, grad, moment_first, moment_second, ql, qr,
    new_weight, update, first_new, second_new,
    qr_all, g_all, ql_all, t_all, p_send, p_recv, b_part, b_send, b_recv, b_all,
    d_acc, d_send, d_recv, send_sem, recv_sem,
):
    row, col = lax.axis_index("row"), lax.axis_index("col")
    xl, y = lax.div(row, 4), lax.rem(row, 4)
    z, u = lax.div(col, 4), lax.rem(col, 4)
    xh, k = lax.div(u, 2), lax.rem(u, 2)

    def ring(value, shift, size):
        return lax.rem(value + (shift + size), size)

    u_core = xh * 2 + (1 - k)
    u_far = (1 - xh) * 2 + k
    u_cross = (1 - xh) * 2 + (1 - k)
    z_at = lambda s: ring(z, s, 8)
    row_at = lambda side, s: (xl if side == 0 else 1 - xl) * 4 + ring(y, s, 4)
    to_core = (row, z * 4 + u_core)
    to_far = (row, z * 4 + u_far)
    to_cross = (row, z * 4 + u_cross)
    to_z = {s: (row, z_at(s) * 4 + u) for s in (1, -1)}
    to_y = {s: (row_at(0, s), col) for s in (1, -1)}
    to_x = (row_at(1, 0), col)

    started = []

    def send(src, dst, to):
        n = len(started)
        copy = pltpu.make_async_remote_copy(
            src_ref=src, dst_ref=dst, send_sem=send_sem.at[n], recv_sem=recv_sem.at[n],
            device_id=to, device_id_type=pl.DeviceIdType.MESH,
        )
        copy.start()
        started.append(copy)
        return copy

    def lanes(index, width):
        return pl.ds(pl.multiple_of(index * width, width), width)

    barrier = pltpu.get_barrier_semaphore()
    partners = (to_core, to_far, to_cross, to_z[1], to_z[-1], to_y[1], to_y[-1], to_x)
    for partner in partners:
        pl.semaphore_signal(
            barrier, inc=1, device_id=partner, device_id_type=pl.DeviceIdType.MESH
        )
    pl.semaphore_wait(barrier, len(partners))

    near_in = send(qr.at[:, lanes(u_core, COLS)], qr_all.at[row, u], to_core)
    far_in = send(qr.at[:, lanes(u_far, COLS)], qr_all.at[row, u], to_far)
    cross_in = send(qr.at[:, lanes(u_cross, COLS)], qr_all.at[row, u], to_cross)
    g_core = send(grad, g_all.at[:, lanes(u, COLS)], to_core)
    ql_core = send(ql, ql_all.at[z, xh, k], to_core)
    qr_all[row, u] = qr[:, lanes(u, COLS)]
    g_all[:, lanes(u, COLS)] = grad[...]
    ql_all[z, xh, k] = ql[...]

    def piece(owner, pair):
        return qr_all.at[owner, pl.ds(pair * 2, 2)]

    def part(owner, pair, n):
        return qr_all.at[owner, pair * 2 + n]

    def spread(ref, owner):
        view = ref(owner)
        return [send(view, view, to_x), send(view, view, to_y[1]), send(view, view, to_y[-1])]

    near_in.wait_recv()
    near = spread(lambda o: piece(o, xh), row)
    far_in.wait_recv()
    cross_in.wait_recv()
    far = spread(lambda o: piece(o, 1 - xh), row)
    g_far = send(grad, g_all.at[:, lanes(u, COLS)], to_far)
    ql_far = send(ql, ql_all.at[z, xh, k], to_far)

    later = []

    def spread_second(first, pair):
        other = row_at(1, 0)
        first[0].wait_recv()
        for s in (1, -1):
            later.append(send(piece(other, pair), piece(other, pair), to_y[s]))
        halves = []
        for n, s in enumerate((1, -1)):
            first[1 + n].wait_recv()
            view = part(row_at(0, -s), pair, n)
            halves.append(send(view, view, to_y[s]))
        return halves

    def spread_third(halves, pair):
        for n in range(2):
            halves[n].wait_recv()
            view = part(row_at(0, 2), pair, n)
            later.append(send(view, view, to_x))

    near_half = spread_second(near, xh)
    ql_core.wait_recv()
    ql_far.wait_recv()
    view = ql_all.at[z, 1 - xh, k]
    later.append(send(view, view, to_core))
    view = ql_all.at[z, :, k]
    ql_step = [send(view, view, to_z[s]) for s in (1, -1)]
    g_core.wait_recv()
    g_far.wait_recv()
    view = g_all.at[:, lanes(u_far, COLS)]
    later.append(send(view, view, to_core))

    def ql_forward(step, now):
        out = []
        for n, s in enumerate((1, -1)):
            now[n].wait_recv()
            owner = z_at(-s * step)
            view = ql_all.at[owner, :, k]
            if step < 3:
                out.append(send(view, view, to_z[s]))
            if step == 3:
                half = ql_all.at[owner, n, k]
                out.append(send(half, half, to_z[s]))
            if step == 4:
                view = ql_all.at[owner, n, k]
            later.append(send(view, view, to_core))
        return out

    far_half = spread_second(far, 1 - xh)
    ql_step = ql_forward(1, ql_step)
    spread_third(near_half, xh)
    ql_step = ql_forward(2, ql_step)
    spread_third(far_half, 1 - xh)
    ql_step = ql_forward(3, ql_step)
    ql_forward(4, ql_step)
    for copy in later:
        copy.wait_recv()

    def right_part(owner):
        return jnp.dot(
            g_all[...], qr_all[owner].reshape(4 * COLS, COLS), preferred_element_type=f32
        )

    cut = ROWS // 2
    halves = (pl.ds(0, cut), pl.ds(cut, cut))
    columns = (pl.ds(0, HALF), pl.ds(HALF, HALF))
    signs = (1, -1)
    term = right_part(z_at(4)).astype(bf16)
    moving = {}
    for n, s in enumerate(signs):
        p_send[n, 3, halves[n]] = term[n * cut : (n + 1) * cut]
    for h in range(2):
        for n, s in enumerate(signs):
            moving[n, h] = send(
                p_send.at[n, 3, halves[n], columns[h]],
                p_recv.at[n, 3, halves[n], columns[h]],
                to_z[s],
            )
    for stage in (3, 2, 1):
        for n, s in enumerate(signs):
            term = right_part(z_at(s * stage))
            for h in range(2):
                moving[n, h].wait_recv()
                lane = slice(h * HALF, (h + 1) * HALF)
                if stage == 3:
                    rows = slice(n * cut, (n + 1) * cut)
                    rest = slice((1 - n) * cut, (2 - n) * cut)
                    total = term[rows, lane] + p_recv[n, 3, halves[n], columns[h]].astype(f32)
                    p_send[n, 2, halves[n], columns[h]] = total.astype(bf16)
                    p_send[n, 2, halves[1 - n], columns[h]] = term[rest, lane].astype(bf16)
                else:
                    total = term[:, lane] + p_recv[n, stage, :, columns[h]].astype(f32)
                    p_send[n, stage - 1, :, columns[h]] = total.astype(bf16)
                moving[n, h] = send(
                    p_send.at[n, stage - 1, :, columns[h]],
                    p_recv.at[n, stage - 1, :, columns[h]],
                    to_z[s],
                )
    term = right_part(z)
    t_first = {}
    for h in range(2):
        for n in range(2):
            moving[n, h].wait_recv()
        total = term[:, h * HALF : (h + 1) * HALF]
        for n in range(2):
            total = total + p_recv[n, 0, :, columns[h]].astype(f32)
        t_all[row, :, columns[h]] = total.astype(bf16)
        t_first[h] = spread(lambda o: t_all.at[o, :, columns[h]], row)

    t_half, t_later = {}, {}
    for h in range(2):
        t_later[h] = []
        t_first[h][0].wait_recv()
        view = t_all.at[row_at(1, 0), :, columns[h]]
        for s in signs:
            t_later[h].append(send(view, view, to_y[s]))
        t_half[h] = []
        for n, s in enumerate(signs):
            t_first[h][1 + n].wait_recv()
            view = t_all.at[row_at(0, -s), halves[n], columns[h]]
            t_half[h].append(send(view, view, to_y[s]))
    for h in range(2):
        for n in range(2):
            t_half[h][n].wait_recv()
            view = t_all.at[row_at(0, 2), halves[n], columns[h]]
            t_later[h].append(send(view, view, to_x))

    def back_recv(slot, h, rows=slice(None)):
        return b_recv[slot, rows, columns[h]].astype(f32)

    def back_send(slot, h, value, to):
        b_send[slot, :, columns[h]] = value.astype(bf16)
        return send(b_send.at[slot, :, columns[h]], b_recv.at[slot, :, columns[h]], to)

    n8, n45, n67, n23, n1 = {}, {}, {}, {}, {}
    for h in range(2):
        for copy in t_later[h]:
            copy.wait_recv()
        rotated = jnp.zeros((ROWS, HALF), f32)
        for owner in range(8):
            rotated += lax.dot_general(
                ql_all[owner].reshape(ROWS, ROWS), t_all[owner, :, columns[h]],
                (((0,), (0,)), ((), ())), preferred_element_type=f32,
            )
        first = beta_first * moment_first[:, columns[h]] + (1.0 - beta_first) * rotated
        second = (
            beta_second * moment_second[:, columns[h]] + (1.0 - beta_second) * rotated * rotated
        )
        first_new[:, columns[h]] = first
        second_new[:, columns[h]] = second
        step = (
            first / correct_first / (jnp.sqrt(second / correct_second) + epsilon)
        ).astype(bf16)

        def back(owner):
            return jnp.dot(
                ql_all[owner].reshape(ROWS, ROWS), step, preferred_element_type=f32
            )

        n8[h] = back_send(0, h, back(row_at(1, 2)), to_x)
        n45[h] = [back_send(1 + n, h, back(row_at(1, s)), to_y[s]) for n, s in enumerate(signs)]
        for slot, owner in enumerate((row_at(0, 2), row_at(0, 1), row_at(0, -1), row_at(1, 0), row)):
            b_part[slot, :, columns[h]] = back(owner)
    for h in range(2):
        n8[h].wait_recv()
        total = b_part[0, :, columns[h]] + back_recv(0, h)
        b_send[3, :, columns[h]] = total.astype(bf16)
        n67[h] = [
            send(b_send.at[3, halves[n], columns[h]], b_recv.at[3, halves[n], columns[h]], to_y[-s])
            for n, s in enumerate(signs)
        ]
    for h in range(2):
        for n in range(2):
            n45[h][n].wait_recv()
        total = b_part[3, :, columns[h]] + back_recv(1, h) + back_recv(2, h)
        n1[h] = back_send(4, h, total, to_x)
        n23[h] = []
        for n, s in enumerate(signs):
            n67[h][1 - n].wait_recv()
            slot = 5 + n
            rows = halves[1 - n]
            total = b_part[1 + n, rows, columns[h]] + b_recv[3, rows, columns[h]].astype(f32)
            b_send[slot, rows, columns[h]] = total.astype(bf16)
            rows = halves[n]
            b_send[slot, rows, columns[h]] = b_part[1 + n, rows, columns[h]].astype(bf16)
            n23[h].append(
                send(b_send.at[slot, :, columns[h]], b_recv.at[slot, :, columns[h]], to_y[s])
            )
    e_step = {}
    for h in range(2):
        n1[h].wait_recv()
        for n in range(2):
            n23[h][n].wait_recv()
        total = b_part[4, :, columns[h]] + back_recv(4, h) + back_recv(5, h) + back_recv(6, h)
        b_all[z, :, columns[h]] = total.astype(bf16)
        view = b_all.at[z, :, columns[h]]
        for n, s in enumerate(signs):
            e_step[n, h] = send(view, view, to_z[s])

    def direction_part(owner, rows=slice(None)):
        return lax.dot_general(
            b_all[owner, rows], qr_all[owner].reshape(4 * COLS, COLS),
            (((1,), (1,)), ((), ())), preferred_element_type=f32,
        )

    d_acc[...] = direction_part(z)
    for stage in (1, 2, 3):
        for h in range(2):
            for n, s in enumerate(signs):
                e_step[n, h].wait_recv()
                owner = z_at(-s * stage)
                if stage < 3:
                    view = b_all.at[owner, :, columns[h]]
                else:
                    view = b_all.at[owner, halves[n], columns[h]]
                e_step[n, h] = send(view, view, to_z[s])
        for s in signs:
            d_acc[...] += direction_part(z_at(-s * stage))
    for n in range(2):
        for h in range(2):
            e_step[n, h].wait_recv()
        d_acc[halves[n]] += direction_part(z_at(4), halves[n])

    for m in range(2):
        d_send[m] = d_acc[:, lanes(2 * m + (1 - k), COLS)].astype(bf16)
    d_core = send(d_send.at[pl.ds(0, 2)], d_recv.at[pl.ds(0, 2)], to_core)
    d_core.wait_recv()
    total = d_acc[:, lanes(u_far, COLS)] + d_recv[1 - xh].astype(f32)
    d_send[2] = total.astype(bf16)
    d_far = send(d_send.at[2], d_recv.at[2], to_far)
    total = d_acc[:, lanes(u, COLS)] + d_recv[xh].astype(f32)
    d_far.wait_recv()
    direction = total + d_recv[2].astype(f32)
    update[...] = direction.astype(bf16)
    wide = weight[...].astype(f32)
    new_weight[...] = (wide - learn_rate * (direction + decay_rate * wide)).astype(bf16)
    for copy in started:
        copy.wait_send()


def on_device(weight, grad, moment_first, moment_second, basis_left, basis_right):
    block = (ROWS, COLS)
    vmem = pl.BlockSpec(memory_space=pltpu.VMEM)
    return pl.pallas_call(
        kernel,
        name="soap_step",
        out_shape=(
            jax.ShapeDtypeStruct(block, bf16),
            jax.ShapeDtypeStruct(block, bf16),
            jax.ShapeDtypeStruct(block, f32),
            jax.ShapeDtypeStruct(block, f32),
        ),
        in_specs=[vmem] * 6,
        out_specs=(vmem,) * 4,
        scratch_shapes=[
            pltpu.VMEM((8, 4, COLS, COLS), bf16),
            pltpu.VMEM((ROWS, 4 * COLS), bf16),
            pltpu.VMEM((8, 2, 2, 128, ROWS), bf16),
            pltpu.VMEM((8,) + block, bf16),
            pltpu.VMEM((2, 4) + block, bf16),
            pltpu.VMEM((2, 4) + block, bf16),
            pltpu.VMEM((5,) + block, f32),
            pltpu.VMEM((7,) + block, bf16),
            pltpu.VMEM((7,) + block, bf16),
            pltpu.VMEM((8,) + block, bf16),
            pltpu.VMEM((ROWS, 4 * COLS), f32),
            pltpu.VMEM((3,) + block, bf16),
            pltpu.VMEM((3,) + block, bf16),
            pltpu.SemaphoreType.DMA((N_MSG,)),
            pltpu.SemaphoreType.DMA((N_MSG,)),
        ],
        compiler_params=pltpu.CompilerParams(
            collective_id=0, has_side_effects=True, vmem_limit_bytes=56 * 2**20
        ),
        cost_estimate=pl.CostEstimate(
            flops=6 * 2**30, bytes_accessed=4 * 2**20, transcendentals=0
        ),
    )(weight, grad, moment_first, moment_second, basis_left, basis_right)


def solution(mesh):
    spec = P("row", "col")
    turned = P("col", "row")
    return jax.shard_map(
        on_device,
        mesh=mesh,
        in_specs=(spec, spec, spec, spec, turned, turned),
        out_specs=(spec,) * 4,
        check_vma=False,
    )
```

time: 531 us -> 168 us (0.32)
  waiting for transfers between devices: 490 us -> 0 us
  Pallas kernels: 0 us -> 162 us
  matrix products: 22.6 us -> 0 us
  between operations: 14.2 us -> 0.66 us
    all_gather x4 -> x0, waiting for transfers between devices: 296 us -> none  [the longest x1 106 us: on_device(): lax.all_gather(left_back, 'col', axis=1, tiled=True)]
    reduce_scatter x2 -> x0, waiting for transfers between devices: 193 us -> none  [the longest x1 148 us: on_device(): lax.psum_scatter(lax.dot_general(right_rows, grad, (((0,), (1,)), ((), ()...]
    pallas_call x0 -> x1, Pallas kernels: none -> 162 us  [on_device(): pl.pallas_call(kernel, name='soap_step', out_shape=(jax.ShapeDtypeStruct(...]
    dot_general x4 -> x0, matrix products: 22.6 us -> none  [the longest x1 7.83 us: on_device(): lax.dot_general(right_rows, grad, (((0,), (1,)), ((), ())), preferred_ele...]
  transfers between devices with their start and end apart: 6 -> 0, of which waited for: 6 -> 0; matrix products, arithmetic and copies ran while one was open for 0% -> 0% of each run, Pallas kernels for 0% -> 0%
where the time goes in v1:
time: 168 us
  Pallas kernels  162 us (96%)
  local copies, waits for them, and re-layouts  4.47 us (3%)
    pallas_call x1, Pallas kernels, on_device(): pl.pallas_call(kernel, name='soap_step', out_shape=(jax.ShapeDtypeStruct(...  162 us
    unnamed x10, local copies, waits for them, and re-layouts  4.47 us

profile of v1, /device:TPU:1, one launch (start us, length us, event | category | flops | bytes accessed | tf_op | source)
XLA Modules:
  0.0 167.6 jit_solution(18414405542394485909)
XLA Ops:
  0.6 162.5 %soap_step.1 = (bf16[512,256]{1,0:T(8,128)(2,1)}, bf16[512,256]{1,0:T(8,128)(2,1)}, f32[512,256]{1,0:T(8,128)}, f32[512,256]{1,0:T(8,128)}) custom-call(bf16[512,256]{1,0:T(8,128)(2,1)} %weight.1, bf16[512,256]{1,0:T(8,128)(2,1)} %grad.1, f32[512,256]{1,0:T(8,128)} %moment_first.1, f32[512,256]{1,0:T(8,128)} %moment_second.1, bf16[128,512]{1,0:T(8,128)(2,1)} %ql.1, ...), custom_call_target="tpu_custom_call" | custom-call | flops 6442450944 | bytes 4194304 | tf_op jit(solution)/shard_map/soap_step/pallas_call | solution.py:344
  163.1 0.0 copy-start.2
  163.1 0.0 copy-start.1
  163.1 1.7 %copy.14 = bf16[512,256]{1,0:T(8,128)(2,1)} copy(bf16[512,256]{1,0:T(8,128)(2,1)} %get-tuple-element.8) | data formatting | bytes 524288
  164.9 0.0 copy-done.2
  164.9 0.7 copy.15
  165.6 0.0 copy-done.1
  165.6 0.0 copy-start
  165.6 0.8 copy.16
  166.4 0.4 copy-done
  166.8 0.8 copy.17
Async XLA Ops:
  163.1 1.8 %copy-start.2 = (bf16[512,256]{1,0:T(8,128)(2,1)S(1)}, bf16[512,256]{1,0:T(8,128)(2,1)}, u32[]{:S(2)}) copy-start(bf16[512,256]{1,0:T(8,128)(2,1)} %get-tuple-element.9) | copy-start | bytes 786436
  163.1 2.5 %copy-start.1 = (f32[512,256]{1,0:T(8,128)S(1)}, f32[512,256]{1,0:T(8,128)}, u32[]{:S(2)}) copy-start(f32[512,256]{1,0:T(8,128)} %get-tuple-element.10) | copy-start | bytes 1572868
  165.6 1.2 copy-start

commit v2 on v1

--- a/solution.py
+++ b/solution.py
@@ -74,61 +74,42 @@
     near_in = send(qr.at[:, lanes(u_core, COLS)], qr_all.at[row, u], to_core)
     far_in = send(qr.at[:, lanes(u_far, COLS)], qr_all.at[row, u], to_far)
     cross_in = send(qr.at[:, lanes(u_cross, COLS)], qr_all.at[row, u], to_cross)
+    ql_far = send(ql, ql_all.at[z, xh, k], to_far)
+    ql_core = send(ql, ql_all.at[z, xh, k], to_core)
     g_core = send(grad, g_all.at[:, lanes(u, COLS)], to_core)
-    ql_core = send(ql, ql_all.at[z, xh, k], to_core)
     qr_all[row, u] = qr[:, lanes(u, COLS)]
     g_all[:, lanes(u, COLS)] = grad[...]
     ql_all[z, xh, k] = ql[...]
 
-    def piece(owner, pair):
-        return qr_all.at[owner, pl.ds(pair * 2, 2)]
-
-    def part(owner, pair, n):
-        return qr_all.at[owner, pair * 2 + n]
-
     def spread(ref, owner):
         view = ref(owner)
         return [send(view, view, to_x), send(view, view, to_y[1]), send(view, view, to_y[-1])]
 
-    near_in.wait_recv()
-    near = spread(lambda o: piece(o, xh), row)
-    far_in.wait_recv()
-    cross_in.wait_recv()
-    far = spread(lambda o: piece(o, 1 - xh), row)
-    g_far = send(grad, g_all.at[:, lanes(u, COLS)], to_far)
-    ql_far = send(ql, ql_all.at[z, xh, k], to_far)
-
-    later = []
-
-    def spread_second(first, pair):
-        other = row_at(1, 0)
+    def piece(pair):
+        return lambda owner: qr_all.at[owner, pl.ds(pair * 2, 2)]
+
+    def spread_other(first, ref):
         first[0].wait_recv()
-        for s in (1, -1):
-            later.append(send(piece(other, pair), piece(other, pair), to_y[s]))
-        halves = []
+        view = ref(row_at(1, 0))
+        return [send(view, view, to_y[s]) for s in (1, -1)]
+
+    def spread_half(first, ref):
+        out = []
         for n, s in enumerate((1, -1)):
             first[1 + n].wait_recv()
-            view = part(row_at(0, -s), pair, n)
-            halves.append(send(view, view, to_y[s]))
-        return halves
-
-    def spread_third(halves, pair):
-        for n in range(2):
-            halves[n].wait_recv()
-            view = part(row_at(0, 2), pair, n)
-            later.append(send(view, view, to_x))
-
-    near_half = spread_second(near, xh)
-    ql_core.wait_recv()
-    ql_far.wait_recv()
-    view = ql_all.at[z, 1 - xh, k]
-    later.append(send(view, view, to_core))
-    view = ql_all.at[z, :, k]
-    ql_step = [send(view, view, to_z[s]) for s in (1, -1)]
-    g_core.wait_recv()
-    g_far.wait_recv()
-    view = g_all.at[:, lanes(u_far, COLS)]
-    later.append(send(view, view, to_core))
+            view = ref(row_at(0, -s), n)
+            out.append(send(view, view, to_y[s]))
+        return out
+
+    def spread_last(half, ref):
+        out = []
+        for n in range(2):
+            half[n].wait_recv()
+            view = ref(row_at(0, 2), n)
+            out.append(send(view, view, to_x))
+        return out
+
+    ql_later = []
 
     def ql_forward(step, now):
         out = []
@@ -143,17 +124,36 @@
                 out.append(send(half, half, to_z[s]))
             if step == 4:
                 view = ql_all.at[owner, n, k]
-            later.append(send(view, view, to_core))
+            ql_later.append(send(view, view, to_core))
         return out
 
-    far_half = spread_second(far, 1 - xh)
+    def part(pair):
+        return lambda owner, n: qr_all.at[owner, pair * 2 + n]
+
+    near_in.wait_recv()
+    near = spread(piece(xh), row)
+    far_in.wait_recv()
+    cross_in.wait_recv()
+    far = spread(piece(1 - xh), row)
+    g_far = send(grad, g_all.at[:, lanes(u, COLS)], to_far)
+    near_half = spread_half(near, part(xh))
+    ql_far.wait_recv()
+    view = ql_all.at[z, 1 - xh, k]
+    ql_later.append(send(view, view, to_core))
+    view = ql_all.at[z, :, k]
+    ql_step = [send(view, view, to_z[s]) for s in (1, -1)]
+    far_half = spread_half(far, part(1 - xh))
+    near_other = spread_other(near, piece(xh))
     ql_step = ql_forward(1, ql_step)
-    spread_third(near_half, xh)
+    near_last = spread_last(near_half, part(xh))
+    far_other = spread_other(far, piece(1 - xh))
+    far_last = spread_last(far_half, part(1 - xh))
     ql_step = ql_forward(2, ql_step)
-    spread_third(far_half, 1 - xh)
+    g_far.wait_recv()
+    view = g_all.at[:, lanes(u_far, COLS)]
+    g_cross = send(view, view, to_core)
     ql_step = ql_forward(3, ql_step)
-    ql_forward(4, ql_step)
-    for copy in later:
+    for copy in [g_core, g_cross] + near_other + far_other + near_last + far_last:
         copy.wait_recv()
 
     def right_part(owner):
@@ -207,6 +207,7 @@
         t_all[row, :, columns[h]] = total.astype(bf16)
         t_first[h] = spread(lambda o: t_all.at[o, :, columns[h]], row)
 
+    ql_forward(4, ql_step)
     t_half, t_later = {}, {}
     for h in range(2):
         t_later[h] = []
@@ -233,6 +234,8 @@
         return send(b_send.at[slot, :, columns[h]], b_recv.at[slot, :, columns[h]], to)
 
     n8, n45, n67, n23, n1 = {}, {}, {}, {}, {}
+    for copy in [ql_core] + ql_later:
+        copy.wait_recv()
     for h in range(2):
         for copy in t_later[h]:
             copy.wait_recv()

time: 168 us -> 148 us (0.88)
  Pallas kernels: 162 us -> 143 us
    pallas_call x1, Pallas kernels: 162 us -> 143 us  [on_device(): pl.pallas_call(kernel, name='soap_step', out_shape=(jax.ShapeDtypeStruct(...]
where the time goes in v2:
time: 148 us
  Pallas kernels  143 us (97%)
  local copies, waits for them, and re-layouts  4.47 us (3%)
    pallas_call x1, Pallas kernels, on_device(): pl.pallas_call(kernel, name='soap_step', out_shape=(jax.ShapeDtypeStruct(...  143 us
    unnamed x10, local copies, waits for them, and re-layouts  4.47 us

profile of v2, /device:TPU:1, one launch (start us, length us, event | category | flops | bytes accessed | tf_op | source)
XLA Modules:
  0.0 148.0 jit_solution(604545187371812590)
XLA Ops:
  0.6 142.9 %soap_step.1 = (bf16[512,256]{1,0:T(8,128)(2,1)}, bf16[512,256]{1,0:T(8,128)(2,1)}, f32[512,256]{1,0:T(8,128)}, f32[512,256]{1,0:T(8,128)}) custom-call(bf16[512,256]{1,0:T(8,128)(2,1)} %weight.1, bf16[512,256]{1,0:T(8,128)(2,1)} %grad.1, f32[512,256]{1,0:T(8,128)} %moment_first.1, f32[512,256]{1,0:T(8,128)} %moment_second.1, bf16[128,512]{1,0:T(8,128)(2,1)} %ql.1, ...), custom_call_target="tpu_custom_call" | custom-call | flops 6442450944 | bytes 4194304 | tf_op jit(solution)/shard_map/soap_step/pallas_call | solution.py:347
  143.5 0.0 copy-start.2
  143.5 0.0 copy-start.1
  143.5 1.7 %copy.14 = bf16[512,256]{1,0:T(8,128)(2,1)} copy(bf16[512,256]{1,0:T(8,128)(2,1)} %get-tuple-element.8) | data formatting | bytes 524288
  145.3 0.0 copy-done.2
  145.3 0.7 copy.15
  146.0 0.0 copy-done.1
  146.0 0.0 copy-start
  146.0 0.8 copy.16
  146.8 0.4 copy-done
  147.2 0.8 copy.17
Async XLA Ops:
  143.5 1.8 %copy-start.2 = (bf16[512,256]{1,0:T(8,128)(2,1)S(1)}, bf16[512,256]{1,0:T(8,128)(2,1)}, u32[]{:S(2)}) copy-start(bf16[512,256]{1,0:T(8,128)(2,1)} %get-tuple-element.9) | copy-start | bytes 786436
  143.5 2.5 %copy-start.1 = (f32[512,256]{1,0:T(8,128)S(1)}, f32[512,256]{1,0:T(8,128)}, u32[]{:S(2)}) copy-start(f32[512,256]{1,0:T(8,128)} %get-tuple-element.10) | copy-start | bytes 1572868
  146.0 1.2 copy-start

commit v3 on v0

v3 whole, which is shorter than its diff:
```python
import jax
import jax.numpy as jnp
from jax import lax
from jax.experimental import pallas as pl
from jax.experimental.pallas import tpu as pltpu
from jax.sharding import PartitionSpec as P

beta_first = 0.9
beta_second = 0.95
correct_first = 1.0 - 0.9**10
correct_second = 1.0 - 0.95**10
epsilon = 1e-08
learn_rate = 0.001
decay_rate = 0.1

ROWS = 512
COLS = 256
HALF = 128
CUT = ROWS // 2
N_MSG = 256
SIGNS = (1, -1)
LANES = (pl.ds(0, HALF), pl.ds(HALF, HALF))
PARTS = (pl.ds(0, CUT), pl.ds(CUT, CUT))
ALL = pl.ds(0, ROWS)

f32 = jnp.float32
bf16 = jnp.bfloat16

RATE = {"core": 2.0e-6, "far": 22.3e-6, "x": 22.3e-6, "y": 22.3e-6, "z": 22.3e-6}
RANK = {"ql": 0.4, "g": 0.5}
for _h in range(2):
    for _kind in ("qr", "p", "t", "b", "e"):
        RANK[_kind, _h] = float(_h)
C_PARTS, D_PARTS = 2, 2
AHEAD = 1.5
DELAY = {"core": 1.0, "far": 3.7, "x": 2.2, "y": 2.2, "z": 2.2}


class Moving:
    def __init__(self, copy):
        self.copy, self.arrival, self.here = copy, None, False

    def wait(self):
        if not self.here:
            self.copy.wait_recv()
        self.here = True


class Task:
    def __init__(self, steps):
        self.steps, self.waits, self.done = steps, (), False


class Order:
    def __init__(self, send_sem, recv_sem):
        self.send_sem, self.recv_sem = send_sem, recv_sem
        self.now, self.free, self.queues = 0.0, {}, {}
        self.count, self.started, self.tasks = 0, [], []

    def send(self, src, dst, target, rank=0.0):
        to, link, side = target
        n = self.count
        self.count += 1
        copy = pltpu.make_async_remote_copy(
            src_ref=src, dst_ref=dst, send_sem=self.send_sem.at[n],
            recv_sem=self.recv_sem.at[n], device_id=to, device_id_type=pl.DeviceIdType.MESH,
        )
        size = 2
        for extent in dst.shape:
            size *= extent
        move = Moving(copy)
        key = ("x" if link == "far" else link, side)
        queue = self.queues.setdefault(key, [])
        queue.append((rank, n, link, size, move))
        if link == "core":
            self.issue(key)
        return move

    def issue(self, key):
        queue = self.queues[key]
        entry = min(queue, key=lambda item: item[:2])
        queue.remove(entry)
        link, size, move = entry[2:]
        move.copy.start()
        self.started.append(move.copy)
        self.free[key] = max(self.now, self.free.get(key, 0.0)) + size * RATE[link]
        move.arrival = self.free[key] + DELAY[link]

    def work(self, us):
        self.now += us

    def spawn(self, steps):
        task = Task(steps)
        self.tasks.append(task)
        self.step(task)
        return task

    def step(self, task):
        try:
            task.waits = next(task.steps)
        except StopIteration:
            task.done = True
            self.tasks.remove(task)

    def ready(self, task):
        time = 0.0
        for item in task.waits:
            if isinstance(item, Task):
                if not item.done:
                    return None
            elif item.arrival is None:
                return None
            else:
                time = max(time, item.arrival)
        return time

    def run(self):
        while self.tasks:
            events = []
            for n, task in enumerate(self.tasks):
                time = self.ready(task)
                if time is not None:
                    events.append((max(time, self.now), 1, time, n, task))
            for key, queue in self.queues.items():
                if queue:
                    time = max(self.now, self.free.get(key, 0.0) - AHEAD)
                    events.append((time, 0, 0.0, key, None))
            self.now, _, _, key, task = min(events, key=lambda event: event[:3])
            if task is None:
                self.issue(key)
                continue
            for item in task.waits:
                if isinstance(item, Moving):
                    item.wait()
            self.step(task)


def kernel(
    weight, grad, moment_first, moment_second, ql, qr,
    new_weight, update, first_new, second_new,
    qr_all, g_all, ql_all, t_all, r_acc, step_all, p_part, p_send, p_recv,
    b_part, b_send, b_recv, b_all, d_acc, d_send, d_recv, send_sem, recv_sem,
):
    row, col = lax.axis_index("row"), lax.axis_index("col")
    xl, y = lax.div(row, 4), lax.rem(row, 4)
    z, u = lax.div(col, 4), lax.rem(col, 4)
    xh, k = lax.div(u, 2), lax.rem(u, 2)

    def ring(value, shift, size):
        return lax.rem(value + (shift + size), size)

    def z_at(shift):
        return ring(z, shift, 8)

    def row_at(side, shift):
        return (xl if side == 0 else 1 - xl) * 4 + ring(y, shift, 4)

    u_core = xh * 2 + (1 - k)
    u_far = (1 - xh) * 2 + k
    u_cross = (1 - xh) * 2 + (1 - k)
    to_core = ((row, z * 4 + u_core), "core", 0)
    to_far = ((row, z * 4 + u_far), "far", 0)
    to_cross = ((row, z * 4 + u_cross), "far", 0)
    to_x = ((row_at(1, 0), col), "x", 0)
    to_y = {s: ((row_at(0, s), col), "y", s) for s in SIGNS}
    to_z = {s: ((row, z_at(s) * 4 + u), "z", s) for s in SIGNS}

    barrier = pltpu.get_barrier_semaphore()
    partners = (to_core, to_far, to_cross, to_z[1], to_z[-1], to_y[1], to_y[-1], to_x)
    for partner in partners:
        pl.semaphore_signal(
            barrier, inc=1, device_id=partner[0], device_id_type=pl.DeviceIdType.MESH
        )
    pl.semaphore_wait(barrier, len(partners))

    order = Order(send_sem, recv_sem)
    send, spawn, work = order.send, order.spawn, order.work

    def block(index, h=None):
        if h is None:
            return pl.ds(pl.multiple_of(index * COLS, COLS), COLS)
        return pl.ds(pl.multiple_of(index * COLS + h * HALF, HALF), HALF)

    def same(view, target, rank=0.0):
        return send(view, view, target, rank)

    def gather_row(full, half, arrived, rank, last_y=False):
        view = full(row)
        to_side = same(view, to_x, rank)
        first = [same(view, to_y[s], rank) for s in SIGNS]
        arrived(row, None)

        def side():
            yield [to_side]
            other = row_at(1, 0)
            view = full(other)
            copies = [same(view, to_y[s], rank) for s in SIGNS]
            arrived(other, None)
            for n, (copy, s) in enumerate(zip(copies, SIGNS)):
                yield [copy]
                arrived(row_at(1, -s), None)
                if last_y:
                    copies.append(same(half(row_at(1, -s), n), to_y[s], rank))
            for n, copy in enumerate(copies[2:]):
                yield [copy]
                arrived(row_at(1, 2), n)

        def along(n, s):
            yield [first[n]]
            view = half(row_at(0, -s), n)
            copy = same(view, to_y[s], rank)
            arrived(row_at(0, -s), None)
            yield [copy]
            if not last_y:
                view = half(row_at(0, 2), n)
                copy = same(view, to_x, rank)
            arrived(row_at(0, 2), n)
            if not last_y:
                yield [copy]
                arrived(row_at(1, 2), n)

        tasks = [spawn(along(n, s)) for n, s in enumerate(SIGNS)]
        return [spawn(side())] + tasks

    qr_tasks = {}

    def qr_pair(h, copies, pair, last_y=False):
        yield copies
        tasks = gather_row(
            lambda owner: qr_all.at[owner, pl.ds(pair * 2, 2), :, LANES[h]],
            lambda owner, n: qr_all.at[owner, pair * 2 + n, :, LANES[h]],
            lambda owner, n: None,
            RANK["qr", h],
            last_y,
        )
        yield tasks

    def qr_send(h, to_u, target):
        return send(qr.at[:, block(to_u, h)], qr_all.at[row, u, :, LANES[h]], target, RANK["qr", h])

    far = {}
    far[0] = [qr_send(0, u_far, to_far), qr_send(0, u_cross, to_cross)]
    near = [qr_send(h, u_core, to_core) for h in range(2)]
    ql_far = send(ql, ql_all.at[z, xh, k], to_far, RANK["ql"])
    far[1] = [qr_send(1, u_far, to_far), qr_send(1, u_cross, to_cross)]
    ql_core = send(ql, ql_all.at[z, xh, k], to_core)
    g_core = send(grad, g_all.at[:, block(u)], to_core)
    qr_all[row, u] = qr[:, block(u)]
    g_all[:, block(u)] = grad[...]
    ql_all[z, xh, k] = ql[...]

    def start_right():
        tasks = [spawn(qr_pair(0, [near[0]], xh))]
        tasks.append(spawn(qr_pair(0, far[0], 1 - xh, True)))
        g_far = [
            send(grad.at[rows], g_all.at[rows, block(u)], to_far, RANK["g"]) for rows in PARTS
        ]
        spawn(start_second())
        g_cross = []
        for copy, rows in zip(g_far, PARTS):
            yield [copy]
            g_cross.append(same(g_all.at[rows, block(u_far)], to_core))
        yield tasks + [g_core] + g_cross

    def start_second():
        qr_tasks[1] = [spawn(qr_pair(1, [near[1]], xh)), spawn(qr_pair(1, far[1], 1 - xh, True))]
        yield qr_tasks[1]

    ql_copies = [ql_core]

    def ql_chain(which):
        block_of = xh if which == 0 else 1 - xh
        if which == 1:
            yield [ql_far]
            ql_copies.append(same(ql_all.at[z, block_of, k], to_core))

        def along(n, s):
            move = same(ql_all.at[z, block_of, k], to_z[s], RANK["ql"])
            for step in (1, 2, 3, 4):
                if step == 4 and n != which:
                    break
                yield [move]
                view = ql_all.at[z_at(-s * step), block_of, k]
                if step < 3 or (step == 3 and n == which):
                    move = same(view, to_z[s], RANK["ql"])
                ql_copies.append(same(view, to_core))

        yield [spawn(along(n, s)) for n, s in enumerate(SIGNS)]

    def gather_left():
        yield [spawn(ql_chain(which)) for which in range(2)]
        yield ql_copies

    def right_part(owner, h):
        work(0.3)
        return jnp.dot(
            g_all[...], qr_all[owner, :, :, LANES[h]].reshape(4 * COLS, HALF),
            preferred_element_type=f32,
        )

    def sum_z(h):
        sends = {}

        def go(n, m, stage):
            return send(
                p_send.at[n, stage, PARTS[m], LANES[h]],
                p_recv.at[n, stage, PARTS[m], LANES[h]],
                to_z[SIGNS[n]],
                RANK["p", h],
            )

        term = right_part(z_at(4), h).astype(bf16)
        for n in range(2):
            p_send[n, 3, PARTS[n], LANES[h]] = term[n * CUT : (n + 1) * CUT]
            sends[n, n] = go(n, n, 3)
        for n, s in enumerate(SIGNS):
            term = right_part(z_at(3 * s), h)
            p_part[n, 3, :, LANES[h]] = term
            p_send[n, 2, PARTS[1 - n], LANES[h]] = term[(1 - n) * CUT : (2 - n) * CUT].astype(bf16)
            sends[n, 1 - n] = go(n, 1 - n, 2)
        for stage in (2, 1):
            for n, s in enumerate(SIGNS):
                p_part[n, stage, :, LANES[h]] = right_part(z_at(s * stage), h)
        p_part[0, 0, :, LANES[h]] = right_part(z, h)
        last = {}

        def along(n, m):
            move = sends[n, m]
            for stage in (3, 2, 1) if m == n else (2, 1):
                yield [move]
                total = p_part[n, stage, PARTS[m], LANES[h]]
                total = total + p_recv[n, stage, PARTS[m], LANES[h]].astype(f32)
                p_send[n, stage - 1, PARTS[m], LANES[h]] = total.astype(bf16)
                work(0.1)
                move = go(n, m, stage - 1)
            last[n, m] = move

        def arrive(m):
            yield chains[m]
            yield [last[n, m] for n in range(2)]
            total = p_part[0, 0, PARTS[m], LANES[h]]
            for n in range(2):
                total = total + p_recv[n, 0, PARTS[m], LANES[h]].astype(f32)
            t_all[row, PARTS[m], LANES[h]] = total.astype(bf16)
            work(0.1)

        chains = [[spawn(along(n, m)) for n in range(2)] for m in range(2)]
        b_done[h] = [spawn(arrive(m)) for m in range(2)]
        yield b_done[h] if C_PARTS == 1 else []

    def rotate(h, owner, first, size):
        work(0.05 + 0.15 * size / ROWS)
        r_acc[:, LANES[h]] += lax.dot_general(
            ql_all[owner].reshape(ROWS, ROWS)[first : first + size],
            t_all[owner, pl.ds(first, size), LANES[h]],
            (((0,), (0,)), ((), ())), preferred_element_type=f32,
        )

    def gather_rotate(h):
        r_acc[:, LANES[h]] = jnp.zeros((ROWS, HALF), f32)
        size = ROWS // C_PARTS
        waiting = []

        def put(owner, first, size):
            if left_task.done:
                rotate(h, owner, first, size)
            else:
                waiting.append((owner, first, size))

        def part(m):
            if C_PARTS == 2:
                yield [b_done[h][m]]

            def arrived(owner, n):
                if n is None:
                    put(owner, m * size, size)
                else:
                    put(owner, m * size + n * (size // 2), size // 2)

            yield gather_row(
                lambda owner: t_all.at[owner, pl.ds(m * size, size), LANES[h]],
                lambda owner, n: t_all.at[
                    owner, pl.ds(m * size + n * (size // 2), size // 2), LANES[h]
                ],
                arrived,
                RANK["t", h],
            )

        tasks = [spawn(part(m)) for m in range(C_PARTS)]
        yield [left_task]
        for item in waiting:
            rotate(h, *item)
        waiting.clear()
        yield tasks

    def sum_row(h):
        rotated = r_acc[:, LANES[h]]
        first = beta_first * moment_first[:, LANES[h]] + (1.0 - beta_first) * rotated
        second = (
            beta_second * moment_second[:, LANES[h]] + (1.0 - beta_second) * rotated * rotated
        )
        first_new[:, LANES[h]] = first
        second_new[:, LANES[h]] = second
        step_all[:, LANES[h]] = (
            first / correct_first / (jnp.sqrt(second / correct_second) + epsilon)
        ).astype(bf16)
        work(0.3)

        size = ROWS // D_PARTS

        def back(owner, m):
            work(0.25 / D_PARTS)
            return jnp.dot(
                ql_all[owner].reshape(ROWS, ROWS)[m * size : (m + 1) * size],
                step_all[:, LANES[h]],
                preferred_element_type=f32,
            )

        def came(slot, rows):
            return b_recv[slot, rows, LANES[h]].astype(f32)

        def own(slot, rows):
            return b_part[slot, rows, LANES[h]]

        def go(slot, target, rows):
            return send(
                b_send.at[slot, rows, LANES[h]], b_recv.at[slot, rows, LANES[h]], target,
                RANK["b", h],
            )

        spans = [pl.ds(m * size, size) for m in range(D_PARTS)]
        opposite, side = [], []
        for m in range(D_PARTS):
            b_send[0, spans[m], LANES[h]] = back(row_at(1, 2), m).astype(bf16)
            opposite.append(go(0, to_x, spans[m]))
        for m in range(D_PARTS):
            side.append([])
            for n, s in enumerate(SIGNS):
                b_send[1 + n, spans[m], LANES[h]] = back(row_at(1, s), m).astype(bf16)
                side[m].append(go(1 + n, to_y[s], spans[m]))
        owners = (row_at(0, 2), row_at(0, 1), row_at(0, -1), row_at(1, 0), row)
        for slot, owner in enumerate(owners):
            for m in range(D_PARTS):
                b_part[slot, spans[m], LANES[h]] = back(owner, m)

        def reduce(m):
            last, after = [], []
            pieces = [pl.ds(m * size + n * (size // 2), size // 2) for n in range(2)]

            def across():
                yield [opposite[m]]
                total = own(0, spans[m]) + came(0, spans[m])
                b_send[3, spans[m], LANES[h]] = total.astype(bf16)
                work(0.1)
                turned = [go(3, to_y[-s], pieces[n]) for n, s in enumerate(SIGNS)]
                for n, s in enumerate(SIGNS):
                    after.append(spawn(along(n, s, turned[1 - n])))

            def along(n, s, move):
                yield [move]
                rows, rest = pieces[1 - n], pieces[n]
                total = own(1 + n, rows) + came(3, rows)
                b_send[5 + n, rows, LANES[h]] = total.astype(bf16)
                b_send[5 + n, rest, LANES[h]] = own(1 + n, rest).astype(bf16)
                work(0.1)
                last.append(go(5 + n, to_y[s], spans[m]))

            def beside():
                yield side[m]
                total = own(3, spans[m]) + came(1, spans[m]) + came(2, spans[m])
                b_send[4, spans[m], LANES[h]] = total.astype(bf16)
                work(0.1)
                last.append(go(4, to_x, spans[m]))

            yield [spawn(across()), spawn(beside())]
            yield after
            yield last
            total = own(4, spans[m])
            for slot in (4, 5, 6):
                total = total + came(slot, spans[m])
            b_all[z, spans[m], LANES[h]] = total.astype(bf16)
            work(0.1)

        d_done[h] = [spawn(reduce(m)) for m in range(D_PARTS)]
        yield d_done[h] if D_PARTS == 1 else []

    def direction_part(owner, rows):
        work(0.4 if rows is ALL else 0.2)
        return lax.dot_general(
            b_all[owner, rows], qr_all[owner].reshape(4 * COLS, COLS),
            (((1,), (1,)), ((), ())), preferred_element_type=f32,
        )

    b_done, d_done = {}, {}
    seen = set()
    final = {}

    def add_direction(owner, what):
        if what in seen:
            if what == 0:
                d_acc[...] = direction_part(owner, ALL)
                seen.add("own")
            else:
                assert "own" in seen
                d_acc[...] += direction_part(owner, ALL)
        seen.add(what)

    def gather_z(h):
        count = {}

        def come(owner, what):
            count[what] = count.get(what, 0) + 1
            if count[what] == 2:
                add_direction(owner, what)

        def along(n, m):
            if D_PARTS == 2:
                yield [d_done[h][m]]
            s = SIGNS[n]
            if n == 0:
                come(z, 0)
            view = b_all.at[z, PARTS[m], LANES[h]]
            move = same(view, to_z[s], RANK["e", h])
            for stage in (1, 2, 3):
                yield [move]
                owner = z_at(-s * stage)
                if stage < 3 or m == n:
                    view = b_all.at[owner, PARTS[m], LANES[h]]
                    move = same(view, to_z[s], RANK["e", h])
                come(owner, (n, stage))
            if m == n:
                final[h, n] = move

        yield [spawn(along(n, m)) for m in range(2) for n in range(2)]

    def pipeline(h):
        yield [right_task]
        if h == 1:
            yield qr_tasks[1]
        for part in (sum_z, gather_rotate, sum_row, gather_z):
            yield [spawn(part(h))]

    def finish(a):
        rows = PARTS[a]
        yield pipelines
        yield [final[0, a], final[1, a]]
        d_acc[rows] += direction_part(z_at(4), rows)
        for m in range(2):
            d_send[m, rows] = d_acc[rows, block(2 * m + (1 - k))].astype(bf16)
        core = send(d_send.at[pl.ds(0, 2), rows], d_recv.at[pl.ds(0, 2), rows], to_core)
        yield [core]
        total = d_acc[rows, block(u_far)] + d_recv[1 - xh, rows].astype(f32)
        d_send[2, rows] = total.astype(bf16)
        far_copy = send(d_send.at[2, rows], d_recv.at[2, rows], to_far)
        yield [far_copy]
        total = d_acc[rows, block(u)] + d_recv[xh, rows].astype(f32)
        direction = total + d_recv[2, rows].astype(f32)
        update[rows] = direction.astype(bf16)
        wide = weight[rows].astype(f32)
        new_weight[rows] = (wide - learn_rate * (direction + decay_rate * wide)).astype(bf16)

    left_task = spawn(gather_left())
    right_task = spawn(start_right())
    pipelines = [spawn(pipeline(h)) for h in range(2)]
    for a in range(2):
        spawn(finish(a))
    order.run()
    for copy in order.started:
        copy.wait_send()


def on_device(weight, grad, moment_first, moment_second, basis_left, basis_right):
    block = (ROWS, COLS)
    vmem = pl.BlockSpec(memory_space=pltpu.VMEM)
    return pl.pallas_call(
        kernel,
        name="soap_step",
        out_shape=(
            jax.ShapeDtypeStruct(block, bf16),
            jax.ShapeDtypeStruct(block, bf16),
            jax.ShapeDtypeStruct(block, f32),
            jax.ShapeDtypeStruct(block, f32),
        ),
        in_specs=[vmem] * 6,
        out_specs=(vmem,) * 4,
        scratch_shapes=[
            pltpu.VMEM((8, 4, COLS, COLS), bf16),
            pltpu.VMEM((ROWS, 4 * COLS), bf16),
            pltpu.VMEM((8, 2, 2, 128, ROWS), bf16),
            pltpu.VMEM((8,) + block, bf16),
            pltpu.VMEM(block, f32),
            pltpu.VMEM(block, bf16),
            pltpu.VMEM((2, 4) + block, f32),
            pltpu.VMEM((2, 4) + block, bf16),
            pltpu.VMEM((2, 4) + block, bf16),
            pltpu.VMEM((5,) + block, f32),
            pltpu.VMEM((7,) + block, bf16),
            pltpu.VMEM((7,) + block, bf16),
            pltpu.VMEM((8,) + block, bf16),
            pltpu.VMEM((ROWS, 4 * COLS), f32),
            pltpu.VMEM((3,) + block, bf16),
            pltpu.VMEM((3,) + block, bf16),
            pltpu.SemaphoreType.DMA((N_MSG,)),
            pltpu.SemaphoreType.DMA((N_MSG,)),
        ],
        compiler_params=pltpu.CompilerParams(
            collective_id=0, has_side_effects=True, vmem_limit_bytes=56 * 2**20
        ),
        cost_estimate=pl.CostEstimate(
            flops=6 * 2**30, bytes_accessed=4 * 2**20, transcendentals=0
        ),
    )(weight, grad, moment_first, moment_second, basis_left, basis_right)


def solution(mesh):
    spec = P("row", "col")
    turned = P("col", "row")
    return jax.shard_map(
        on_device,
        mesh=mesh,
        in_specs=(spec, spec, spec, spec, turned, turned),
        out_specs=(spec,) * 4,
        check_vma=False,
    )
```

time: 531 us -> 136 us (0.26)
  waiting for transfers between devices: 490 us -> 0 us
  Pallas kernels: 0 us -> 131 us
  matrix products: 22.6 us -> 0 us
  between operations: 14.2 us -> 0.66 us
    all_gather x4 -> x0, waiting for transfers between devices: 296 us -> none  [the longest x1 106 us: on_device(): lax.all_gather(left_back, 'col', axis=1, tiled=True)]
    reduce_scatter x2 -> x0, waiting for transfers between devices: 193 us -> none  [the longest x1 148 us: on_device(): lax.psum_scatter(lax.dot_general(right_rows, grad, (((0,), (1,)), ((), ()...]
    pallas_call x0 -> x1, Pallas kernels: none -> 131 us  [on_device(): pl.pallas_call(kernel, name='soap_step', out_shape=(jax.ShapeDtypeStruct(...]
    dot_general x4 -> x0, matrix products: 22.6 us -> none  [the longest x1 7.83 us: on_device(): lax.dot_general(right_rows, grad, (((0,), (1,)), ((), ())), preferred_ele...]
  transfers between devices with their start and end apart: 6 -> 0, of which waited for: 6 -> 0; matrix products, arithmetic and copies ran while one was open for 0% -> 0% of each run, Pallas kernels for 0% -> 0%
where the time goes in v3:
time: 136 us
  Pallas kernels  131 us (96%)
  local copies, waits for them, and re-layouts  4.47 us (3%)
    pallas_call x1, Pallas kernels, on_device(): pl.pallas_call(kernel, name='soap_step', out_shape=(jax.ShapeDtypeStruct(...  131 us
    unnamed x10, local copies, waits for them, and re-layouts  4.47 us

profile of v3, /device:TPU:1, one launch (start us, length us, event | category | flops | bytes accessed | tf_op | source)
XLA Modules:
  0.0 136.1 jit_solution(9223854221867541028)
XLA Ops:
  0.6 131.0 %soap_step.1 = (bf16[512,256]{1,0:T(8,128)(2,1)}, bf16[512,256]{1,0:T(8,128)(2,1)}, f32[512,256]{1,0:T(8,128)}, f32[512,256]{1,0:T(8,128)}) custom-call(bf16[512,256]{1,0:T(8,128)(2,1)} %weight.1, bf16[512,256]{1,0:T(8,128)(2,1)} %grad.1, f32[512,256]{1,0:T(8,128)} %moment_first.1, f32[512,256]{1,0:T(8,128)} %moment_second.1, bf16[128,512]{1,0:T(8,128)(2,1)} %ql.1, ...), custom_call_target="tpu_custom_call" | custom-call | flops 6442450944 | bytes 4194304 | tf_op jit(solution)/shard_map/soap_step/pallas_call | solution.py:575
  131.7 0.0 copy-start.2
  131.7 0.0 copy-start.1
  131.7 1.7 %copy.14 = bf16[512,256]{1,0:T(8,128)(2,1)} copy(bf16[512,256]{1,0:T(8,128)(2,1)} %get-tuple-element.8) | data formatting | bytes 524288
  133.4 0.0 copy-done.2
  133.4 0.7 copy.15
  134.1 0.0 copy-done.1
  134.1 0.0 copy-start
  134.1 0.8 copy.16
  134.9 0.4 copy-done
  135.4 0.8 copy.17
Async XLA Ops:
  131.7 1.8 %copy-start.2 = (bf16[512,256]{1,0:T(8,128)(2,1)S(1)}, bf16[512,256]{1,0:T(8,128)(2,1)}, u32[]{:S(2)}) copy-start(bf16[512,256]{1,0:T(8,128)(2,1)} %get-tuple-element.9) | copy-start | bytes 786436
  131.7 2.5 %copy-start.1 = (f32[512,256]{1,0:T(8,128)S(1)}, f32[512,256]{1,0:T(8,128)}, u32[]{:S(2)}) copy-start(f32[512,256]{1,0:T(8,128)} %get-tuple-element.10) | copy-start | bytes 1572868
  134.1 1.2 copy-start

commit v4 on v3

v4 whole, which is shorter than its diff:
```python
import jax
import jax.numpy as jnp
from jax import lax
from jax.experimental import pallas as pl
from jax.experimental.pallas import tpu as pltpu
from jax.sharding import PartitionSpec as P

beta_first = 0.9
beta_second = 0.95
correct_first = 1.0 - 0.9**10
correct_second = 1.0 - 0.95**10
epsilon = 1e-08
learn_rate = 0.001
decay_rate = 0.1

ROWS = 512
COLS = 256
HALF = 128
CUT = ROWS // 2
N_MSG = 300
SIGNS = (1, -1)
LANES = (pl.ds(0, HALF), pl.ds(HALF, HALF))
PARTS = (pl.ds(0, CUT), pl.ds(CUT, CUT))
ALL = pl.ds(0, ROWS)

f32 = jnp.float32
bf16 = jnp.bfloat16

RATE = {"core": 2.0e-6, "far": 22.3e-6, "x": 22.3e-6, "o": 22.3e-6, "y": 22.3e-6, "z": 22.3e-6}
RANK = {
    ("b", 0, 0, 0): -0.18, ("b", 0, 0, 1): -0.65, ("b", 0, 0, 2): -0.39, ("b", 0, 0, 3): -0.91,
    ("b", 0, 0, 4): 0.67, ("b", 0, 0, 5): -0.92, ("b", 0, 0, 6): 0.98, ("b", 0, 1, 0): 0.16,
    ("b", 0, 1, 1): 0.81, ("b", 0, 1, 2): -0.06, ("b", 0, 1, 3): 1.51, ("b", 0, 1, 4): -1.33,
    ("b", 0, 1, 5): 1.19, ("b", 0, 1, 6): -0.62, ("b", 1, 0, 0): 0.32, ("b", 1, 0, 1): 1.55,
    ("b", 1, 0, 2): -2.48, ("b", 1, 0, 3): 2.07, ("b", 1, 0, 4): 1.13, ("b", 1, 0, 5): -0.97,
    ("b", 1, 0, 6): -0.87, ("b", 1, 1, 0): -1.47, ("b", 1, 1, 1): -0.04, ("b", 1, 1, 2): 0.2,
    ("b", 1, 1, 3): 1.23, ("b", 1, 1, 4): 1.88, ("b", 1, 1, 5): 0.01, ("b", 1, 1, 6): 1.46,
    ("e", 0, 0, 0): 1.54, ("e", 0, 0, 1): 1.16, ("e", 0, 0, 2): 0.74, ("e", 0, 0, 3): 1.72,
    ("e", 0, 1, 0): 1.51, ("e", 0, 1, 1): 1.48, ("e", 0, 1, 2): 0.56, ("e", 0, 1, 3): 1.21,
    ("e", 1, 0, 0): 0.6, ("e", 1, 0, 1): -1.51, ("e", 1, 0, 2): 1.5, ("e", 1, 0, 3): 0.68,
    ("e", 1, 1, 0): -0.72, ("e", 1, 1, 1): 1.3, ("e", 1, 1, 2): -1.36, ("e", 1, 1, 3): 1.4,
    ("g", 0): 1.9, ("g", 1): 1.66, ("in", 0, 1): 1.24, ("in", 0, 2): -0.35, ("in", 0, 3): -0.51,
    ("in", 1, 1): -0.25, ("in", 1, 2): 1.17, ("in", 1, 3): 0.87, ("p", 0, False, 0): 0.24,
    ("p", 0, False, 1): 0.17, ("p", 0, False, 2): 1.9, ("p", 0, True, 0): 0.04,
    ("p", 0, True, 1): -0.44, ("p", 0, True, 2): 0.56, ("p", 0, True, 3): 0.71,
    ("p", 1, False, 0): 1.38, ("p", 1, False, 1): -0.52, ("p", 1, False, 2): -0.31,
    ("p", 1, True, 0): 0.13, ("p", 1, True, 1): -1.84, ("p", 1, True, 2): -0.28,
    ("p", 1, True, 3): -0.71, ("ql", "far"): 1.1, ("ql", 0, 0): 0.26, ("ql", 0, 1): 0.35,
    ("ql", 0, 2): -0.36, ("ql", 0, 3): 0.14, ("ql", 1, 0): 1.57, ("ql", 1, 1): -0.3,
    ("ql", 1, 2): 0.35, ("ql", 1, 3): -0.01, ("qr", 0, 0, "half"): -0.0,
    ("qr", 0, 0, "last"): 2.11, ("qr", 0, 0, "other"): -0.37, ("qr", 0, 0, "x"): 1.32,
    ("qr", 0, 0, "y"): 2.12, ("qr", 0, 1, "half"): -0.48, ("qr", 0, 1, "last"): -0.36,
    ("qr", 0, 1, "other"): 1.89, ("qr", 0, 1, "x"): -0.92, ("qr", 0, 1, "y"): -0.3,
    ("qr", 0, 2, "half"): 1.42, ("qr", 0, 2, "last"): 2.57, ("qr", 0, 2, "other"): 0.41,
    ("qr", 0, 2, "x"): 0.3, ("qr", 0, 2, "y"): -1.32, ("qr", 0, 3, "half"): -0.09,
    ("qr", 0, 3, "last"): 1.18, ("qr", 0, 3, "other"): 1.24, ("qr", 0, 3, "x"): -1.07,
    ("qr", 0, 3, "y"): -1.71, ("qr", 1, 0, "half"): 7.28, ("qr", 1, 0, "last"): -1.82,
    ("qr", 1, 0, "other"): 1.17, ("qr", 1, 0, "x"): 7.28, ("qr", 1, 0, "y"): -0.79,
    ("qr", 1, 1, "half"): 7.42, ("qr", 1, 1, "last"): 1.45, ("qr", 1, 1, "other"): -0.13,
    ("qr", 1, 1, "x"): 6.0, ("qr", 1, 1, "y"): 2.65, ("qr", 1, 2, "half"): -1.43,
    ("qr", 1, 2, "last"): 2.51, ("qr", 1, 2, "other"): 0.5, ("qr", 1, 2, "x"): 11.2,
    ("qr", 1, 2, "y"): 7.65, ("qr", 1, 3, "half"): 2.25, ("qr", 1, 3, "last"): 0.65,
    ("qr", 1, 3, "other"): -0.04, ("qr", 1, 3, "x"): 13.6, ("qr", 1, 3, "y"): 6.81,
    ("t", 0, 0, "half"): 0.18, ("t", 0, 0, "last"): -1.08, ("t", 0, 0, "other"): 0.69,
    ("t", 0, 0, "x"): -0.17, ("t", 0, 0, "y"): 0.09, ("t", 0, 1, "half"): 0.94,
    ("t", 0, 1, "last"): -0.66, ("t", 0, 1, "other"): -0.03, ("t", 0, 1, "x"): -1.31,
    ("t", 0, 1, "y"): 0.58, ("t", 1, 0, "half"): 0.24, ("t", 1, 0, "last"): 1.46,
    ("t", 1, 0, "other"): 3.9, ("t", 1, 0, "x"): 2.96, ("t", 1, 0, "y"): 3.43,
    ("t", 1, 1, "half"): 2.67, ("t", 1, 1, "last"): 1.27, ("t", 1, 1, "other"): 1.79,
    ("t", 1, 1, "x"): 2.08, ("t", 1, 1, "y"): 0.27,
}


def rank_of(*key):
    if key in RANK:
        return RANK[key]
    if key[0] in ("ql", "g"):
        return 0.45
    return float(key[1])


LAST_Y = {("qr", 0, 2), ("t", 0, 0), ("t", 0, 1), ("t", 1, 1)}
C_PARTS, D_PARTS = 2, 2
Z_PARTS = 2
ZPARTS = [pl.ds(m * (ROWS // Z_PARTS), ROWS // Z_PARTS) for m in range(Z_PARTS)]
AHEAD = 1.5
DELAY = {"core": 1.0, "far": 3.7, "x": 2.2, "o": 2.2, "y": 2.2, "z": 2.2}


def new_moments(first, second, rotated):
    return (
        beta_first * first + (1.0 - beta_first) * rotated,
        beta_second * second + (1.0 - beta_second) * rotated * rotated,
    )


class Moving:
    def __init__(self, copy):
        self.copy, self.arrival, self.here = copy, None, False

    def wait(self):
        if not self.here:
            self.copy.wait_recv()
        self.here = True


class Task:
    def __init__(self, steps):
        self.steps, self.waits, self.done = steps, (), False


class Order:
    def __init__(self, send_sem, recv_sem):
        self.send_sem, self.recv_sem = send_sem, recv_sem
        self.now, self.free, self.queues = 0.0, {}, {}
        self.count, self.started, self.tasks = 0, [], []

    def send(self, src, dst, target, *key):
        to, link, side = target
        rank = rank_of(*key) if key else 0.0
        n = self.count
        self.count += 1
        copy = pltpu.make_async_remote_copy(
            src_ref=src, dst_ref=dst, send_sem=self.send_sem.at[n],
            recv_sem=self.recv_sem.at[n], device_id=to, device_id_type=pl.DeviceIdType.MESH,
        )
        size = 2
        for extent in dst.shape:
            size *= extent
        move = Moving(copy)
        key = ("x" if link == "far" else link, side)
        queue = self.queues.setdefault(key, [])
        queue.append((rank, n, link, size, move))
        if link == "core":
            self.issue(key)
        return move

    def issue(self, key):
        queue = self.queues[key]
        entry = min(queue, key=lambda item: item[:2])
        queue.remove(entry)
        link, size, move = entry[2:]
        move.copy.start()
        self.now += 0.05
        self.started.append(move.copy)
        self.free[key] = max(self.now, self.free.get(key, 0.0)) + size * RATE[link]
        move.arrival = self.free[key] + DELAY[link]

    def work(self, us):
        self.now += us

    def spawn(self, steps):
        task = Task(steps)
        self.tasks.append(task)
        self.step(task)
        return task

    def step(self, task):
        try:
            task.waits = next(task.steps)
        except StopIteration:
            task.done = True
            self.tasks.remove(task)

    def ready(self, task):
        time = 0.0
        for item in task.waits:
            if isinstance(item, Task):
                if not item.done:
                    return None
            elif item.arrival is None:
                return None
            else:
                time = max(time, item.arrival)
        return time

    def run(self):
        while self.tasks:
            events = []
            for n, task in enumerate(self.tasks):
                time = self.ready(task)
                if time is not None:
                    events.append((max(time, self.now), 1, time, n, task))
            for key, queue in self.queues.items():
                if queue:
                    time = max(self.now, self.free.get(key, 0.0) - AHEAD)
                    events.append((time, 0, 0.0, key, None))
            self.now, _, _, key, task = min(events, key=lambda event: event[:3])
            if task is None:
                self.issue(key)
                continue
            for item in task.waits:
                if isinstance(item, Moving):
                    item.wait()
            self.step(task)


def far_part(n, m):
    return m * 2 // Z_PARTS == n


def kernel(
    grad, moment_first, moment_second, ql, qr, rotated_out, direction_out,
    first_old, second_old, qr_all, g_all, ql_all, t_all, r_acc, step_all, p_part, p_send, p_recv,
    b_part, b_send, b_recv, b_all, d_acc, d_out, d_send, d_recv,
    send_sem, recv_sem, local_sem,
):
    row, col = lax.axis_index("row"), lax.axis_index("col")
    xl, y = lax.div(row, 4), lax.rem(row, 4)
    z, u = lax.div(col, 4), lax.rem(col, 4)
    xh, k = lax.div(u, 2), lax.rem(u, 2)

    def ring(value, shift, size):
        return lax.rem(value + (shift + size), size)

    def z_at(shift):
        return ring(z, shift, 8)

    def row_at(side, shift):
        return (xl if side == 0 else 1 - xl) * 4 + ring(y, shift, 4)

    u_core = xh * 2 + (1 - k)
    u_far = (1 - xh) * 2 + k
    u_cross = (1 - xh) * 2 + (1 - k)
    to_core = ((row, z * 4 + u_core), "core", 0)
    to_far = ((row, z * 4 + u_far), "far", 0)
    to_x = ((row_at(1, 0), col), "x", 0)
    to_other = ((row_at(1, 0), z * 4 + u_far), "o", 0)
    to_cross = ((row_at(1, 0), z * 4 + u_cross), "o", 0)
    to_y = {s: ((row_at(0, s), col), "y", s) for s in SIGNS}
    to_z = {s: ((row, z_at(s) * 4 + u), "z", s) for s in SIGNS}

    def block(index, h=None):
        if h is None:
            return pl.ds(pl.multiple_of(index * COLS, COLS), COLS)
        return pl.ds(pl.multiple_of(index * COLS + h * HALF, HALF), HALF)

    barrier = pltpu.get_barrier_semaphore()
    partners = (to_core, to_far, to_other, to_cross, to_z[1], to_z[-1], to_y[1], to_y[-1], to_x)
    for partner in partners:
        pl.semaphore_signal(
            barrier, inc=1, device_id=partner[0], device_id_type=pl.DeviceIdType.MESH
        )
    local = []

    def move(src, dst):
        copy = pltpu.make_async_copy(src, dst, local_sem.at[len(local)])
        copy.start()
        local.append(copy)
        return copy

    own_copies = [move(qr.at[:, block(u, h)], qr_all.at[h, row, u]) for h in range(2)]
    own_copies.append(move(ql, ql_all.at[z, xh, k]))
    own_copies.append(move(grad, g_all.at[:, block(u)]))
    old_copies = [move(moment_first, first_old), move(moment_second, second_old)]
    pl.semaphore_wait(barrier, len(partners))

    order = Order(send_sem, recv_sem)
    send, spawn, work = order.send, order.spawn, order.work

    def same(view, target, *key):
        return send(view, view, target, *key)

    def gather_row(full, half, arrived, flip, *key):
        last_y = key in LAST_Y

        def at(side, shift):
            return row_at(side if not flip else 1 - side, shift)

        view = full(at(0, 0))
        to_side = same(view, to_x, *key, "x")
        first = [same(view, to_y[s], *key, "y") for s in SIGNS]
        arrived(at(0, 0), None)

        def side():
            yield [to_side]
            other = at(1, 0)
            view = full(other)
            copies = [same(view, to_y[s], *key, "other") for s in SIGNS]
            arrived(other, None)
            for n, (copy, s) in enumerate(zip(copies, SIGNS)):
                yield [copy]
                arrived(at(1, -s), None)
                if last_y:
                    copies.append(same(half(at(1, -s), n), to_y[s], *key, "last"))
            for n, copy in enumerate(copies[2:]):
                yield [copy]
                arrived(at(1, 2), n)

        def along(n, s):
            yield [first[n]]
            view = half(at(0, -s), n)
            copy = same(view, to_y[s], *key, "half")
            arrived(at(0, -s), None)
            yield [copy]
            if not last_y:
                view = half(at(0, 2), n)
                copy = same(view, to_x, *key, "last")
            arrived(at(0, 2), n)
            if not last_y:
                yield [copy]
                arrived(at(1, 2), n)

        tasks = [spawn(along(n, s)) for n, s in enumerate(SIGNS)]
        return [spawn(side())] + tasks

    blocks = (u, u_core, u_far, u_cross)

    def qr_block(h, i):
        if i > 0:
            yield [qr_in[h, i]]
        source = blocks[i]
        yield gather_row(
            lambda owner: qr_all.at[h, owner, source, :],
            lambda owner, n: qr_all.at[h, owner, source, pl.ds(n * HALF, HALF)],
            lambda owner, n: None,
            i > 1,
            "qr", h, i,
        )

    qr_in = {}
    for h in range(2):
        for i, target in ((1, to_core), (2, to_other), (3, to_cross)):
            qr_in[h, i] = send(
                qr.at[:, block(blocks[i], h)], qr_all.at[h, row, u, :], target,
                "in", h, i,
            )
    ql_far = send(ql, ql_all.at[z, xh, k], to_far, "ql", "far")
    g_far = [
        send(grad.at[rows], g_all.at[rows, block(u)], to_far, "g", n)
        for n, rows in enumerate(PARTS)
    ]
    ql_core = send(ql, ql_all.at[z, xh, k], to_core)
    g_core = send(grad, g_all.at[:, block(u)], to_core)
    for copy in own_copies + old_copies:
        copy.wait()

    def gather_right(h):
        yield [spawn(qr_block(h, i)) for i in range(4)]

    def gather_grad():
        g_cross = []
        for copy, rows in zip(g_far, PARTS):
            yield [copy]
            g_cross.append(same(g_all.at[rows, block(u_far)], to_core))
        yield [g_core] + g_cross

    ql_copies = [ql_core]

    def ql_chain(which):
        block_of = xh if which == 0 else 1 - xh
        if which == 1:
            yield [ql_far]
            ql_copies.append(same(ql_all.at[z, block_of, k], to_core))

        def along(n, s):
            move = same(ql_all.at[z, block_of, k], to_z[s], "ql", which, 0)
            for step in (1, 2, 3, 4):
                if step == 4 and n != which:
                    break
                yield [move]
                view = ql_all.at[z_at(-s * step), block_of, k]
                if step < 3 or (step == 3 and n == which):
                    move = same(view, to_z[s], "ql", which, step)
                ql_copies.append(same(view, to_core))

        yield [spawn(along(n, s)) for n, s in enumerate(SIGNS)]

    def gather_left():
        yield [spawn(ql_chain(which)) for which in range(2)]
        yield ql_copies

    def right_part(owner, h):
        work(0.3)
        return jnp.dot(
            g_all[...], qr_all[h, owner, :, :].reshape(4 * COLS, HALF),
            preferred_element_type=f32,
        )

    def sum_z(h):
        sends = {}

        def go(n, m, stage):
            return send(
                p_send.at[h, n, stage, ZPARTS[m]],
                p_recv.at[h, n, stage, ZPARTS[m]],
                to_z[SIGNS[n]],
                "p", h, far_part(n, m), stage,
            )

        term = right_part(z_at(4), h).astype(bf16)
        p_send[h, 0, 3, PARTS[0]] = term[:CUT]
        p_send[h, 1, 3, PARTS[1]] = term[CUT:]
        for m in range(Z_PARTS):
            n = 0 if far_part(0, m) else 1
            sends[n, m] = go(n, m, 3)
        for n, s in enumerate(SIGNS):
            term = right_part(z_at(3 * s), h)
            p_part[h, n, 3, :] = term
            p_send[h, n, 2, PARTS[1 - n]] = term[(1 - n) * CUT : (2 - n) * CUT].astype(bf16)
            for m in range(Z_PARTS):
                if not far_part(n, m):
                    sends[n, m] = go(n, m, 2)
        for stage in (2, 1):
            for n, s in enumerate(SIGNS):
                p_part[h, n, stage, :] = right_part(z_at(s * stage), h)
        p_part[h, 0, 0, :] = right_part(z, h)
        last = {}

        def along(n, m):
            move = sends[n, m]
            for stage in (3, 2, 1) if far_part(n, m) else (2, 1):
                yield [move]
                total = p_part[h, n, stage, ZPARTS[m]]
                total = total + p_recv[h, n, stage, ZPARTS[m]].astype(f32)
                p_send[h, n, stage - 1, ZPARTS[m]] = total.astype(bf16)
                work(0.2 / Z_PARTS)
                move = go(n, m, stage - 1)
            last[n, m] = move

        def arrive(c):
            parts = range(c * Z_PARTS // 2, (c + 1) * Z_PARTS // 2)
            for m in parts:
                yield chains[m]
                yield [last[n, m] for n in range(2)]
                total = p_part[h, 0, 0, ZPARTS[m]]
                for n in range(2):
                    total = total + p_recv[h, n, 0, ZPARTS[m]].astype(f32)
                t_all[h, row, ZPARTS[m]] = total.astype(bf16)
                work(0.2 / Z_PARTS)

        chains = [[spawn(along(n, m)) for n in range(2)] for m in range(Z_PARTS)]
        b_done[h] = [spawn(arrive(c)) for c in range(2)]
        yield b_done[h] if C_PARTS == 1 else []

    def rotate(h, owner, first, size):
        work(0.05 + 0.15 * size / ROWS)
        r_acc[:, LANES[h]] += lax.dot_general(
            ql_all[owner].reshape(ROWS, ROWS)[first : first + size],
            t_all[h, owner, pl.ds(first, size)],
            (((0,), (0,)), ((), ())), preferred_element_type=f32,
        )

    def gather_rotate(h):
        r_acc[:, LANES[h]] = jnp.zeros((ROWS, HALF), f32)
        size = ROWS // C_PARTS
        waiting = []

        def put(owner, first, size):
            if left_task.done:
                rotate(h, owner, first, size)
            else:
                waiting.append((owner, first, size))

        def part(m):
            if C_PARTS == 2:
                yield [b_done[h][m]]

            def arrived(owner, n):
                if n is None:
                    put(owner, m * size, size)
                else:
                    put(owner, m * size + n * (size // 2), size // 2)

            yield gather_row(
                lambda owner: t_all.at[h, owner, pl.ds(m * size, size)],
                lambda owner, n: t_all.at[
                    h, owner, pl.ds(m * size + n * (size // 2), size // 2)
                ],
                arrived,
                False,
                "t", h, m,
            )

        tasks = [spawn(part(m)) for m in range(C_PARTS)]
        yield [left_task]
        for item in waiting:
            rotate(h, *item)
        waiting.clear()
        yield tasks

    def sum_row(h):
        rotated = r_acc[:, LANES[h]]
        out_copies.append(move(r_acc.at[:, LANES[h]], rotated_out.at[:, LANES[h]]))
        first, second = new_moments(first_old[:, LANES[h]], second_old[:, LANES[h]], rotated)
        step_all[:, LANES[h]] = (
            first / correct_first / (jnp.sqrt(second / correct_second) + epsilon)
        ).astype(bf16)
        work(0.3)

        size = ROWS // D_PARTS

        def back(owner, m):
            work(0.25 / D_PARTS)
            return jnp.dot(
                ql_all[owner].reshape(ROWS, ROWS)[m * size : (m + 1) * size],
                step_all[:, LANES[h]],
                preferred_element_type=f32,
            )

        def came(slot, rows):
            return b_recv[h, slot, rows].astype(f32)

        def own(slot, rows):
            return b_part[h, slot, rows]

        def go(slot, target, rows, m):
            return send(
                b_send.at[h, slot, rows], b_recv.at[h, slot, rows], target,
                "b", h, m, slot,
            )

        spans = [pl.ds(m * size, size) for m in range(D_PARTS)]
        opposite, side = [], []
        for m in range(D_PARTS):
            b_send[h, 0, spans[m]] = back(row_at(1, 2), m).astype(bf16)
            opposite.append(go(0, to_x, spans[m], m))
        for m in range(D_PARTS):
            side.append([])
            for n, s in enumerate(SIGNS):
                b_send[h, 1 + n, spans[m]] = back(row_at(1, s), m).astype(bf16)
                side[m].append(go(1 + n, to_y[s], spans[m], m))
        owners = (row_at(0, 2), row_at(0, 1), row_at(0, -1), row_at(1, 0), row)
        for slot, owner in enumerate(owners):
            for m in range(D_PARTS):
                b_part[h, slot, spans[m]] = back(owner, m)

        def reduce(m):
            last, after = [], []
            pieces = [pl.ds(m * size + n * (size // 2), size // 2) for n in range(2)]

            def across():
                yield [opposite[m]]
                total = own(0, spans[m]) + came(0, spans[m])
                b_send[h, 3, spans[m]] = total.astype(bf16)
                work(0.1)
                turned = [go(3, to_y[-s], pieces[n], m) for n, s in enumerate(SIGNS)]
                for n, s in enumerate(SIGNS):
                    after.append(spawn(along(n, s, turned[1 - n])))

            def along(n, s, move):
                yield [move]
                rows, rest = pieces[1 - n], pieces[n]
                total = own(1 + n, rows) + came(3, rows)
                b_send[h, 5 + n, rows] = total.astype(bf16)
                b_send[h, 5 + n, rest] = own(1 + n, rest).astype(bf16)
                work(0.1)
                last.append(go(5 + n, to_y[s], spans[m], m))

            def beside():
                yield side[m]
                total = own(3, spans[m]) + came(1, spans[m]) + came(2, spans[m])
                b_send[h, 4, spans[m]] = total.astype(bf16)
                work(0.1)
                last.append(go(4, to_x, spans[m], m))

            yield [spawn(across()), spawn(beside())]
            yield after
            yield last
            total = own(4, spans[m])
            for slot in (4, 5, 6):
                total = total + came(slot, spans[m])
            b_all[h, z, spans[m]] = total.astype(bf16)
            work(0.1)

        d_done[h] = [spawn(reduce(m)) for m in range(D_PARTS)]
        yield d_done[h] if D_PARTS == 1 else []

    def direction_part(owner, rows):
        work(0.4 if rows is ALL else 0.2)
        left = jnp.concatenate([b_all[h, owner, rows] for h in range(2)], axis=1)
        right = jnp.concatenate(
            [qr_all[h, owner].reshape(4 * COLS, HALF) for h in range(2)], axis=1
        )
        return lax.dot_general(
            left, right, (((1,), (1,)), ((), ())), preferred_element_type=f32
        )

    b_done, d_done = {}, {}
    seen = set()
    final = {}

    def add_direction(owner, what):
        if what in seen:
            if what == 0:
                d_acc[...] = direction_part(owner, ALL)
                seen.add("own")
            else:
                assert "own" in seen
                d_acc[...] += direction_part(owner, ALL)
        seen.add(what)

    def gather_z(h):
        count = {}

        def come(owner, what):
            count[what] = count.get(what, 0) + 1
            if count[what] == Z_PARTS:
                add_direction(owner, what)

        def along(n, m):
            if D_PARTS == 2:
                yield [d_done[h][m * 2 // Z_PARTS]]
            s = SIGNS[n]
            if n == 0:
                come(z, 0)
            view = b_all.at[h, z, ZPARTS[m]]
            move = same(view, to_z[s], "e", h, m, 0)
            for stage in (1, 2, 3):
                yield [move]
                owner = z_at(-s * stage)
                if stage < 3 or far_part(n, m):
                    view = b_all.at[h, owner, ZPARTS[m]]
                    move = same(view, to_z[s], "e", h, m, stage)
                come(owner, (n, stage))
            if far_part(n, m):
                final[h, m] = move

        yield [spawn(along(n, m)) for m in range(Z_PARTS) for n in range(2)]

    def pipeline(h):
        yield [right_tasks[h], grad_task]
        for part in (sum_z, gather_rotate, sum_row, gather_z):
            yield [spawn(part(h))]

    def finish(a):
        rows = PARTS[a]
        yield pipelines
        yield [final[h, m] for h in range(2) for m in range(Z_PARTS) if m * 2 // Z_PARTS == a]
        d_acc[rows] += direction_part(z_at(4), rows)
        for m in range(2):
            d_send[m, rows] = d_acc[rows, block(2 * m + (1 - k))].astype(bf16)
        core = send(d_send.at[pl.ds(0, 2), rows], d_recv.at[pl.ds(0, 2), rows], to_core)
        yield [core]
        total = d_acc[rows, block(u_far)] + d_recv[1 - xh, rows].astype(f32)
        d_send[2, rows] = total.astype(bf16)
        far_copy = send(d_send.at[2, rows], d_recv.at[2, rows], to_far)
        yield [far_copy]
        total = d_acc[rows, block(u)] + d_recv[xh, rows].astype(f32)
        d_out[rows] = total + d_recv[2, rows].astype(f32)
        out_copies.append(move(d_out.at[rows], direction_out.at[rows]))

    out_copies = []
    left_task = spawn(gather_left())
    right_tasks = [spawn(gather_right(h)) for h in range(2)]
    grad_task = spawn(gather_grad())
    pipelines = [spawn(pipeline(h)) for h in range(2)]
    for a in range(2):
        spawn(finish(a))
    order.run()
    for copy in order.started:
        copy.wait_send()
    for copy in out_copies:
        copy.wait()


def on_device(weight, grad, moment_first, moment_second, basis_left, basis_right):
    block = (ROWS, COLS)
    half = (ROWS, HALF)
    anywhere = pl.BlockSpec(memory_space=pl.ANY)
    rotated, direction = pl.pallas_call(
        kernel,
        name="soap_step",
        out_shape=(jax.ShapeDtypeStruct(block, f32), jax.ShapeDtypeStruct(block, f32)),
        in_specs=[anywhere] * 5,
        out_specs=(anywhere,) * 2,
        scratch_shapes=[
            pltpu.VMEM(block, f32),
            pltpu.VMEM(block, f32),
            pltpu.VMEM((2, 8, 4, COLS, HALF), bf16),
            pltpu.VMEM((ROWS, 4 * COLS), bf16),
            pltpu.VMEM((8, 2, 2, 128, ROWS), bf16),
            pltpu.VMEM((2, 8) + half, bf16),
            pltpu.VMEM(block, f32),
            pltpu.VMEM(block, bf16),
            pltpu.VMEM((2, 2, 4) + half, f32),
            pltpu.VMEM((2, 2, 4) + half, bf16),
            pltpu.VMEM((2, 2, 4) + half, bf16),
            pltpu.VMEM((2, 5) + half, f32),
            pltpu.VMEM((2, 7) + half, bf16),
            pltpu.VMEM((2, 7) + half, bf16),
            pltpu.VMEM((2, 8) + half, bf16),
            pltpu.VMEM((ROWS, 4 * COLS), f32),
            pltpu.VMEM(block, f32),
            pltpu.VMEM((3,) + block, bf16),
            pltpu.VMEM((3,) + block, bf16),
            pltpu.SemaphoreType.DMA((N_MSG,)),
            pltpu.SemaphoreType.DMA((N_MSG,)),
            pltpu.SemaphoreType.DMA((16,)),
        ],
        compiler_params=pltpu.CompilerParams(
            collective_id=0, has_side_effects=True, vmem_limit_bytes=56 * 2**20
        ),
        cost_estimate=pl.CostEstimate(
            flops=6 * 2**30, bytes_accessed=4 * 2**20, transcendentals=0
        ),
    )(grad, moment_first, moment_second, basis_left, basis_right)
    first_new, second_new = new_moments(moment_first, moment_second, rotated)
    update = direction.astype(bf16)
    wide = weight.astype(f32)
    new_weight = (wide - learn_rate * (direction + decay_rate * wide)).astype(bf16)
    return new_weight, update, first_new, second_new


def solution(mesh):
    spec = P("row", "col")
    turned = P("col", "row")
    return jax.shard_map(
        on_device,
        mesh=mesh,
        in_specs=(spec, spec, spec, spec, turned, turned),
        out_specs=(spec,) * 4,
        check_vma=False,
    )
```

time: 136 us -> 129 us (0.949)
  Pallas kernels: 131 us -> 125 us
  local copies, waits for them, and re-layouts: 4.47 us -> 0.01 us
  other arithmetic: 0 us -> 2.61 us
    pallas_call x1, Pallas kernels: 131 us -> 125 us  [on_device(): pl.pallas_call(kernel, name='soap_step', out_shape=(jax.ShapeDtypeStruct(...]
    unnamed x10 -> x6, local copies, waits for them, and re-layouts: 4.47 us -> 0.01 us
    add x0 -> x1, other arithmetic: none -> 2.61 us  [new_moments(): beta_second * second + (1.0 - beta_second) * rotated * rotated]
where the time goes in v4:
time: 129 us; the launch traced here: 128 us
  Pallas kernels  125 us (97%)
  other arithmetic  2.61 us (2%)
    pallas_call x1, Pallas kernels, on_device(): pl.pallas_call(kernel, name='soap_step', out_shape=(jax.ShapeDtypeStruct(...  125 us
    add x1, other arithmetic, new_moments(): beta_second * second + (1.0 - beta_second) * rotated * rotated  2.61 us

profile of v4, /device:TPU:1, one launch (start us, length us, event | category | flops | bytes accessed | tf_op | source)
XLA Modules:
  0.0 128.5 jit_solution(15976571317147724552)
XLA Ops:
  0.6 0.0 copy-start.1
  0.6 0.0 copy-start
  0.7 0.0 copy-start.2
  0.7 125.2 %soap_step.1 = (f32[512,256]{1,0:T(8,128)}, f32[512,256]{1,0:T(8,128)}) custom-call(bf16[512,256]{1,0:T(8,128)(2,1)} %grad.1, f32[512,256]{1,0:T(8,128)} %moment_first.1, f32[512,256]{1,0:T(8,128)} %moment_second.1, bf16[128,512]{1,0:T(8,128)(2,1)} %ql.1, bf16[256,1024]{1,0:T(8,128)(2,1)} %qr.1), custom_call_target="tpu_custom_call" | custom-call | flops 6442450944 | bytes 4194304 | tf_op jit(solution)/shard_map/soap_step/pallas_call | solution.py:661
  125.8 0.0 copy-done.1
  125.9 0.0 copy-done
  125.9 0.0 copy-done.2
  125.9 2.6 %fusion.3 = (f32[512,256]{1,0:T(8,128)}, f32[512,256]{1,0:T(8,128)}, bf16[512,256]{1,0:T(8,128)(2,1)}, bf16[512,256]{1,0:T(8,128)(2,1)}) fusion(f32[512,256]{1,0:T(8,128)} %get-tuple-element.7, f32[512,256]{1,0:T(8,128)S(1)} %copy-done.1, f32[512,256]{1,0:T(8,128)S(1)} %copy-done, f32[512,256]{1,0:T(8,128)} %get-tuple-element.6, bf16[512,256]{1,0:T(8,128)(2,1)S(1)} %copy-done.2), kind=kLoop, calls=%fused_computation.6 | loop fusion | flops 1835008 | bytes 3932160 | tf_op jit(solution)/shard_map/add | solution.py:93
Async XLA Ops:
  0.6 125.2 %copy-start.1 = (f32[512,256]{1,0:T(8,128)S(1)}, f32[512,256]{1,0:T(8,128)}, u32[]{:S(2)}) copy-start(f32[512,256]{1,0:T(8,128)} %moment_second.1) | copy-start | bytes 1572868
  0.6 125.2 %copy-start = (f32[512,256]{1,0:T(8,128)S(1)}, f32[512,256]{1,0:T(8,128)}, u32[]{:S(2)}) copy-start(f32[512,256]{1,0:T(8,128)} %moment_first.1) | copy-start | bytes 1572868
  0.7 125.2 %copy-start.2 = (bf16[512,256]{1,0:T(8,128)(2,1)S(1)}, bf16[512,256]{1,0:T(8,128)(2,1)}, u32[]{:S(2)}) copy-start(bf16[512,256]{1,0:T(8,128)(2,1)} %param.6) | copy-start | bytes 786436

commit v5 on v4

--- a/solution.py
+++ b/solution.py
@@ -26,48 +26,48 @@
 f32 = jnp.float32
 bf16 = jnp.bfloat16
 
-RATE = {"core": 2.0e-6, "far": 22.3e-6, "x": 22.3e-6, "o": 22.3e-6, "y": 22.3e-6, "z": 22.3e-6}
+RATE = {"core": 2.0e-6, "far": 18.5e-6, "x": 18.5e-6, "o": 18.5e-6, "y": 18.5e-6, "z": 18.5e-6}
 RANK = {
-    ("b", 0, 0, 0): -0.18, ("b", 0, 0, 1): -0.65, ("b", 0, 0, 2): -0.39, ("b", 0, 0, 3): -0.91,
-    ("b", 0, 0, 4): 0.67, ("b", 0, 0, 5): -0.92, ("b", 0, 0, 6): 0.98, ("b", 0, 1, 0): 0.16,
-    ("b", 0, 1, 1): 0.81, ("b", 0, 1, 2): -0.06, ("b", 0, 1, 3): 1.51, ("b", 0, 1, 4): -1.33,
-    ("b", 0, 1, 5): 1.19, ("b", 0, 1, 6): -0.62, ("b", 1, 0, 0): 0.32, ("b", 1, 0, 1): 1.55,
-    ("b", 1, 0, 2): -2.48, ("b", 1, 0, 3): 2.07, ("b", 1, 0, 4): 1.13, ("b", 1, 0, 5): -0.97,
-    ("b", 1, 0, 6): -0.87, ("b", 1, 1, 0): -1.47, ("b", 1, 1, 1): -0.04, ("b", 1, 1, 2): 0.2,
-    ("b", 1, 1, 3): 1.23, ("b", 1, 1, 4): 1.88, ("b", 1, 1, 5): 0.01, ("b", 1, 1, 6): 1.46,
-    ("e", 0, 0, 0): 1.54, ("e", 0, 0, 1): 1.16, ("e", 0, 0, 2): 0.74, ("e", 0, 0, 3): 1.72,
-    ("e", 0, 1, 0): 1.51, ("e", 0, 1, 1): 1.48, ("e", 0, 1, 2): 0.56, ("e", 0, 1, 3): 1.21,
-    ("e", 1, 0, 0): 0.6, ("e", 1, 0, 1): -1.51, ("e", 1, 0, 2): 1.5, ("e", 1, 0, 3): 0.68,
-    ("e", 1, 1, 0): -0.72, ("e", 1, 1, 1): 1.3, ("e", 1, 1, 2): -1.36, ("e", 1, 1, 3): 1.4,
-    ("g", 0): 1.9, ("g", 1): 1.66, ("in", 0, 1): 1.24, ("in", 0, 2): -0.35, ("in", 0, 3): -0.51,
-    ("in", 1, 1): -0.25, ("in", 1, 2): 1.17, ("in", 1, 3): 0.87, ("p", 0, False, 0): 0.24,
-    ("p", 0, False, 1): 0.17, ("p", 0, False, 2): 1.9, ("p", 0, True, 0): 0.04,
-    ("p", 0, True, 1): -0.44, ("p", 0, True, 2): 0.56, ("p", 0, True, 3): 0.71,
-    ("p", 1, False, 0): 1.38, ("p", 1, False, 1): -0.52, ("p", 1, False, 2): -0.31,
-    ("p", 1, True, 0): 0.13, ("p", 1, True, 1): -1.84, ("p", 1, True, 2): -0.28,
-    ("p", 1, True, 3): -0.71, ("ql", "far"): 1.1, ("ql", 0, 0): 0.26, ("ql", 0, 1): 0.35,
-    ("ql", 0, 2): -0.36, ("ql", 0, 3): 0.14, ("ql", 1, 0): 1.57, ("ql", 1, 1): -0.3,
-    ("ql", 1, 2): 0.35, ("ql", 1, 3): -0.01, ("qr", 0, 0, "half"): -0.0,
-    ("qr", 0, 0, "last"): 2.11, ("qr", 0, 0, "other"): -0.37, ("qr", 0, 0, "x"): 1.32,
-    ("qr", 0, 0, "y"): 2.12, ("qr", 0, 1, "half"): -0.48, ("qr", 0, 1, "last"): -0.36,
-    ("qr", 0, 1, "other"): 1.89, ("qr", 0, 1, "x"): -0.92, ("qr", 0, 1, "y"): -0.3,
-    ("qr", 0, 2, "half"): 1.42, ("qr", 0, 2, "last"): 2.57, ("qr", 0, 2, "other"): 0.41,
-    ("qr", 0, 2, "x"): 0.3, ("qr", 0, 2, "y"): -1.32, ("qr", 0, 3, "half"): -0.09,
-    ("qr", 0, 3, "last"): 1.18, ("qr", 0, 3, "other"): 1.24, ("qr", 0, 3, "x"): -1.07,
-    ("qr", 0, 3, "y"): -1.71, ("qr", 1, 0, "half"): 7.28, ("qr", 1, 0, "last"): -1.82,
-    ("qr", 1, 0, "other"): 1.17, ("qr", 1, 0, "x"): 7.28, ("qr", 1, 0, "y"): -0.79,
-    ("qr", 1, 1, "half"): 7.42, ("qr", 1, 1, "last"): 1.45, ("qr", 1, 1, "other"): -0.13,
-    ("qr", 1, 1, "x"): 6.0, ("qr", 1, 1, "y"): 2.65, ("qr", 1, 2, "half"): -1.43,
-    ("qr", 1, 2, "last"): 2.51, ("qr", 1, 2, "other"): 0.5, ("qr", 1, 2, "x"): 11.2,
-    ("qr", 1, 2, "y"): 7.65, ("qr", 1, 3, "half"): 2.25, ("qr", 1, 3, "last"): 0.65,
-    ("qr", 1, 3, "other"): -0.04, ("qr", 1, 3, "x"): 13.6, ("qr", 1, 3, "y"): 6.81,
-    ("t", 0, 0, "half"): 0.18, ("t", 0, 0, "last"): -1.08, ("t", 0, 0, "other"): 0.69,
-    ("t", 0, 0, "x"): -0.17, ("t", 0, 0, "y"): 0.09, ("t", 0, 1, "half"): 0.94,
-    ("t", 0, 1, "last"): -0.66, ("t", 0, 1, "other"): -0.03, ("t", 0, 1, "x"): -1.31,
-    ("t", 0, 1, "y"): 0.58, ("t", 1, 0, "half"): 0.24, ("t", 1, 0, "last"): 1.46,
-    ("t", 1, 0, "other"): 3.9, ("t", 1, 0, "x"): 2.96, ("t", 1, 0, "y"): 3.43,
-    ("t", 1, 1, "half"): 2.67, ("t", 1, 1, "last"): 1.27, ("t", 1, 1, "other"): 1.79,
-    ("t", 1, 1, "x"): 2.08, ("t", 1, 1, "y"): 0.27,
+    ("b", 0, 0, 0): 0.16, ("b", 0, 0, 1): 0.93, ("b", 0, 0, 2): 1.48, ("b", 0, 0, 3): 2.17,
+    ("b", 0, 0, 4): 1.07, ("b", 0, 0, 5): 1.0, ("b", 0, 0, 6): 1.04, ("b", 0, 1, 0): 2.33,
+    ("b", 0, 1, 1): -0.5, ("b", 0, 1, 2): 1.53, ("b", 0, 1, 3): 1.48, ("b", 0, 1, 4): 1.35,
+    ("b", 0, 1, 5): 2.68, ("b", 0, 1, 6): 1.36, ("b", 1, 0, 0): 0.3, ("b", 1, 0, 1): 1.66,
+    ("b", 1, 0, 2): 1.59, ("b", 1, 0, 3): 1.21, ("b", 1, 0, 4): -0.0, ("b", 1, 0, 5): 1.63,
+    ("b", 1, 0, 6): -0.48, ("b", 1, 1, 0): -1.89, ("b", 1, 1, 1): 1.22, ("b", 1, 1, 2): -0.16,
+    ("b", 1, 1, 3): 0.54, ("b", 1, 1, 4): 0.39, ("b", 1, 1, 5): 1.61, ("b", 1, 1, 6): 1.79,
+    ("e", 0, 0, 0): 2.95, ("e", 0, 0, 1): 0.98, ("e", 0, 0, 2): 1.99, ("e", 0, 0, 3): 1.57,
+    ("e", 0, 1, 0): 1.39, ("e", 0, 1, 1): 1.96, ("e", 0, 1, 2): 0.88, ("e", 0, 1, 3): 3.59,
+    ("e", 1, 0, 0): 3.2, ("e", 1, 0, 1): 1.22, ("e", 1, 0, 2): 0.57, ("e", 1, 0, 3): 0.96,
+    ("e", 1, 1, 0): 1.95, ("e", 1, 1, 1): 0.23, ("e", 1, 1, 2): 2.34, ("e", 1, 1, 3): 1.45,
+    ("g", 0): 0.31, ("g", 1): 0.04, ("in", 0, 1): -1.84, ("in", 0, 2): -1.68, ("in", 0, 3): -1.3,
+    ("in", 1, 1): 1.12, ("in", 1, 2): 1.75, ("in", 1, 3): -0.17, ("p", 0, False, 0): -0.1,
+    ("p", 0, False, 1): 0.94, ("p", 0, False, 2): 1.27, ("p", 0, True, 0): 1.1,
+    ("p", 0, True, 1): 0.11, ("p", 0, True, 2): 1.43, ("p", 0, True, 3): 0.42,
+    ("p", 1, False, 0): 1.6, ("p", 1, False, 1): 1.53, ("p", 1, False, 2): 0.54,
+    ("p", 1, True, 0): 0.04, ("p", 1, True, 1): 1.35, ("p", 1, True, 2): 1.73,
+    ("p", 1, True, 3): -0.26, ("ql", "far"): -0.91, ("ql", 0, 0): 1.68, ("ql", 0, 1): 0.28,
+    ("ql", 0, 2): 0.47, ("ql", 0, 3): 1.43, ("ql", 1, 0): 1.39, ("ql", 1, 1): 0.45,
+    ("ql", 1, 2): 2.27, ("ql", 1, 3): 1.52, ("qr", 0, 0, "half"): 0.14,
+    ("qr", 0, 0, "last"): 0.19, ("qr", 0, 0, "other"): -0.92, ("qr", 0, 0, "x"): -1.36,
+    ("qr", 0, 0, "y"): -1.46, ("qr", 0, 1, "half"): -1.37, ("qr", 0, 1, "last"): -0.46,
+    ("qr", 0, 1, "other"): 0.08, ("qr", 0, 1, "x"): -0.55, ("qr", 0, 1, "y"): 0.7,
+    ("qr", 0, 2, "half"): -0.46, ("qr", 0, 2, "last"): -0.69, ("qr", 0, 2, "other"): -0.25,
+    ("qr", 0, 2, "x"): -1.36, ("qr", 0, 2, "y"): -0.99, ("qr", 0, 3, "half"): 0.51,
+    ("qr", 0, 3, "last"): -0.35, ("qr", 0, 3, "other"): -0.38, ("qr", 0, 3, "x"): -1.78,
+    ("qr", 0, 3, "y"): -0.58, ("qr", 1, 0, "half"): 1.46, ("qr", 1, 0, "last"): 0.35,
+    ("qr", 1, 0, "other"): 0.42, ("qr", 1, 0, "x"): 9.33, ("qr", 1, 0, "y"): 1.0,
+    ("qr", 1, 1, "half"): 1.75, ("qr", 1, 1, "last"): 2.85, ("qr", 1, 1, "other"): 0.94,
+    ("qr", 1, 1, "x"): 4.18, ("qr", 1, 1, "y"): 4.08, ("qr", 1, 2, "half"): 1.21,
+    ("qr", 1, 2, "last"): 2.01, ("qr", 1, 2, "other"): 2.5, ("qr", 1, 2, "x"): 0.99,
+    ("qr", 1, 2, "y"): 10.26, ("qr", 1, 3, "half"): -0.13, ("qr", 1, 3, "last"): 6.48,
+    ("qr", 1, 3, "other"): 0.56, ("qr", 1, 3, "x"): 8.86, ("qr", 1, 3, "y"): 29.39,
+    ("t", 0, 0, "half"): -1.46, ("t", 0, 0, "last"): -0.78, ("t", 0, 0, "other"): 1.41,
+    ("t", 0, 0, "x"): 0.88, ("t", 0, 0, "y"): -1.57, ("t", 0, 1, "half"): 0.62,
+    ("t", 0, 1, "last"): 0.23, ("t", 0, 1, "other"): -2.39, ("t", 0, 1, "x"): 1.15,
+    ("t", 0, 1, "y"): -0.93, ("t", 1, 0, "half"): 0.91, ("t", 1, 0, "last"): 1.81,
+    ("t", 1, 0, "other"): 1.45, ("t", 1, 0, "x"): 1.43, ("t", 1, 0, "y"): 1.3,
+    ("t", 1, 1, "half"): -0.21, ("t", 1, 1, "last"): 1.2, ("t", 1, 1, "other"): 2.4,
+    ("t", 1, 1, "x"): 1.58, ("t", 1, 1, "y"): 1.65,
 }
 
 
@@ -79,12 +79,12 @@
     return float(key[1])
 
 
-LAST_Y = {("qr", 0, 2), ("t", 0, 0), ("t", 0, 1), ("t", 1, 1)}
+LAST_Y = {("qr", 0, 0), ("qr", 0, 3), ("qr", 1, 0), ("qr", 1, 2), ("qr", 1, 3), ("t", 0, 0)}
 C_PARTS, D_PARTS = 2, 2
 Z_PARTS = 2
 ZPARTS = [pl.ds(m * (ROWS // Z_PARTS), ROWS // Z_PARTS) for m in range(Z_PARTS)]
-AHEAD = 1.5
-DELAY = {"core": 1.0, "far": 3.7, "x": 2.2, "o": 2.2, "y": 2.2, "z": 2.2}
+AHEAD = 0.7
+DELAY = {"core": 1.0, "far": 3.7, "x": 2.2, "o": 2.2, "y": 2.8, "z": 2.8}
 
 
 def new_moments(first, second, rotated):
@@ -149,6 +149,18 @@
     def work(self, us):
         self.now += us
 
+    def pause(self):
+        move = Moving(None)
+        move.arrival, move.here = self.now, True
+        return move
+
+    def later(self, function, *tasks):
+        def steps():
+            yield [self.pause()] + list(tasks)
+            function()
+
+        return self.spawn(steps())
+
     def spawn(self, steps):
         task = Task(steps)
         self.tasks.append(task)
@@ -256,7 +268,7 @@
     pl.semaphore_wait(barrier, len(partners))
 
     order = Order(send_sem, recv_sem)
-    send, spawn, work = order.send, order.spawn, order.work
+    send, spawn, work, later = order.send, order.spawn, order.work, order.later
 
     def same(view, target, *key):
         return send(view, view, target, *key)
@@ -332,7 +344,7 @@
     ]
     ql_core = send(ql, ql_all.at[z, xh, k], to_core)
     g_core = send(grad, g_all.at[:, block(u)], to_core)
-    for copy in own_copies + old_copies:
+    for copy in own_copies:
         copy.wait()
 
     def gather_right(h):
@@ -401,16 +413,21 @@
             for m in range(Z_PARTS):
                 if not far_part(n, m):
                     sends[n, m] = go(n, m, 2)
-        for stage in (2, 1):
-            for n, s in enumerate(SIGNS):
-                p_part[h, n, stage, :] = right_part(z_at(s * stage), h)
-        p_part[h, 0, 0, :] = right_part(z, h)
+
+        def compute(n, stage):
+            def run():
+                p_part[h, n, stage] = right_part(z_at(SIGNS[n] * stage), h)
+
+            return later(run)
+
+        computed = {(n, stage): compute(n, stage) for stage in (2, 1) for n in range(2)}
+        computed[0, 0] = compute(0, 0)
         last = {}
 
         def along(n, m):
             move = sends[n, m]
             for stage in (3, 2, 1) if far_part(n, m) else (2, 1):
-                yield [move]
+                yield [move] if stage == 3 else [move, computed[n, stage]]
                 total = p_part[h, n, stage, ZPARTS[m]]
                 total = total + p_recv[h, n, stage, ZPARTS[m]].astype(f32)
                 p_send[h, n, stage - 1, ZPARTS[m]] = total.astype(bf16)
@@ -422,7 +439,7 @@
             parts = range(c * Z_PARTS // 2, (c + 1) * Z_PARTS // 2)
             for m in parts:
                 yield chains[m]
-                yield [last[n, m] for n in range(2)]
+                yield [last[n, m] for n in range(2)] + [computed[0, 0]]
                 total = p_part[h, 0, 0, ZPARTS[m]]
                 for n in range(2):
                     total = total + p_recv[h, n, 0, ZPARTS[m]].astype(f32)
@@ -481,6 +498,8 @@
 
     def sum_row(h):
         rotated = r_acc[:, LANES[h]]
+        while old_copies:
+            old_copies.pop().wait()
         out_copies.append(move(r_acc.at[:, LANES[h]], rotated_out.at[:, LANES[h]]))
         first, second = new_moments(first_old[:, LANES[h]], second_old[:, LANES[h]], rotated)
         step_all[:, LANES[h]] = (
@@ -521,16 +540,21 @@
                 b_send[h, 1 + n, spans[m]] = back(row_at(1, s), m).astype(bf16)
                 side[m].append(go(1 + n, to_y[s], spans[m], m))
         owners = (row_at(0, 2), row_at(0, 1), row_at(0, -1), row_at(1, 0), row)
-        for slot, owner in enumerate(owners):
-            for m in range(D_PARTS):
-                b_part[h, slot, spans[m]] = back(owner, m)
+
+        def compute(slot, m):
+            def run():
+                b_part[h, slot, spans[m]] = back(owners[slot], m)
+
+            return later(run)
+
+        computed = {(slot, m): compute(slot, m) for slot in range(5) for m in range(D_PARTS)}
 
         def reduce(m):
             last, after = [], []
             pieces = [pl.ds(m * size + n * (size // 2), size // 2) for n in range(2)]
 
             def across():
-                yield [opposite[m]]
+                yield [opposite[m], computed[0, m]]
                 total = own(0, spans[m]) + came(0, spans[m])
                 b_send[h, 3, spans[m]] = total.astype(bf16)
                 work(0.1)
@@ -539,7 +563,7 @@
                     after.append(spawn(along(n, s, turned[1 - n])))
 
             def along(n, s, move):
-                yield [move]
+                yield [move, computed[1 + n, m]]
                 rows, rest = pieces[1 - n], pieces[n]
                 total = own(1 + n, rows) + came(3, rows)
                 b_send[h, 5 + n, rows] = total.astype(bf16)
@@ -548,7 +572,7 @@
                 last.append(go(5 + n, to_y[s], spans[m], m))
 
             def beside():
-                yield side[m]
+                yield side[m] + [computed[3, m]]
                 total = own(3, spans[m]) + came(1, spans[m]) + came(2, spans[m])
                 b_send[h, 4, spans[m]] = total.astype(bf16)
                 work(0.1)
@@ -556,7 +580,7 @@
 
             yield [spawn(across()), spawn(beside())]
             yield after
-            yield last
+            yield last + [computed[4, m]]
             total = own(4, spans[m])
             for slot in (4, 5, 6):
                 total = total + came(slot, spans[m])
@@ -577,17 +601,21 @@
         )
 
     b_done, d_done = {}, {}
-    seen = set()
+    seen, added = set(), []
     final = {}
 
     def add_direction(owner, what):
+        def first():
+            d_acc[...] = direction_part(owner, ALL)
+
+        def add():
+            d_acc[...] += direction_part(owner, ALL)
+
         if what in seen:
             if what == 0:
-                d_acc[...] = direction_part(owner, ALL)
-                seen.add("own")
+                added.append(later(first))
             else:
-                assert "own" in seen
-                d_acc[...] += direction_part(owner, ALL)
+                added.append(later(add, added[0]))
         seen.add(what)
 
     def gather_z(h):
@@ -626,6 +654,7 @@
     def finish(a):
         rows = PARTS[a]
         yield pipelines
+        yield added
         yield [final[h, m] for h in range(2) for m in range(Z_PARTS) if m * 2 // Z_PARTS == a]
         d_acc[rows] += direction_part(z_at(4), rows)
         for m in range(2):

time: 129 us -> 124 us (0.961)
  Pallas kernels: 125 us -> 121 us
    pallas_call x1, Pallas kernels: 125 us -> 121 us  [on_device(): pl.pallas_call(kernel, name='soap_step', out_shape=(jax.ShapeDtypeStruct(...]
where the time goes in v5:
time: 124 us
  Pallas kernels  121 us (98%)
  other arithmetic  2.61 us (2%)
    pallas_call x1, Pallas kernels, on_device(): pl.pallas_call(kernel, name='soap_step', out_shape=(jax.ShapeDtypeStruct(...  121 us
    add x1, other arithmetic, new_moments(): beta_second * second + (1.0 - beta_second) * rotated * rotated  2.61 us

profile of v5, /device:TPU:1, one launch (start us, length us, event | category | flops | bytes accessed | tf_op | source)
XLA Modules:
  0.0 124.3 jit_solution(7864668696092044294)
XLA Ops:
  0.6 0.0 copy-start.1
  0.6 0.0 copy-start
  0.7 0.0 copy-start.2
  0.7 121.0 %soap_step.1 = (f32[512,256]{1,0:T(8,128)}, f32[512,256]{1,0:T(8,128)}) custom-call(bf16[512,256]{1,0:T(8,128)(2,1)} %grad.1, f32[512,256]{1,0:T(8,128)} %moment_first.1, f32[512,256]{1,0:T(8,128)} %moment_second.1, bf16[128,512]{1,0:T(8,128)(2,1)} %ql.1, bf16[256,1024]{1,0:T(8,128)(2,1)} %qr.1), custom_call_target="tpu_custom_call" | custom-call | flops 6442450944 | bytes 4194304 | tf_op jit(solution)/shard_map/soap_step/pallas_call | solution.py:690
  121.7 0.0 copy-done.1
  121.7 0.0 copy-done
  121.7 0.0 copy-done.2
  121.7 2.6 %fusion.3 = (f32[512,256]{1,0:T(8,128)}, f32[512,256]{1,0:T(8,128)}, bf16[512,256]{1,0:T(8,128)(2,1)}, bf16[512,256]{1,0:T(8,128)(2,1)}) fusion(f32[512,256]{1,0:T(8,128)} %get-tuple-element.7, f32[512,256]{1,0:T(8,128)S(1)} %copy-done.1, f32[512,256]{1,0:T(8,128)S(1)} %copy-done, f32[512,256]{1,0:T(8,128)} %get-tuple-element.6, bf16[512,256]{1,0:T(8,128)(2,1)S(1)} %copy-done.2), kind=kLoop, calls=%fused_computation.6 | loop fusion | flops 1835008 | bytes 3932160 | tf_op jit(solution)/shard_map/add | solution.py:93
Async XLA Ops:
  0.6 121.1 %copy-start.1 = (f32[512,256]{1,0:T(8,128)S(1)}, f32[512,256]{1,0:T(8,128)}, u32[]{:S(2)}) copy-start(f32[512,256]{1,0:T(8,128)} %moment_second.1) | copy-start | bytes 1572868
  0.6 121.1 %copy-start = (f32[512,256]{1,0:T(8,128)S(1)}, f32[512,256]{1,0:T(8,128)}, u32[]{:S(2)}) copy-start(f32[512,256]{1,0:T(8,128)} %moment_first.1) | copy-start | bytes 1572868
  0.7 121.1 %copy-start.2 = (bf16[512,256]{1,0:T(8,128)(2,1)S(1)}, bf16[512,256]{1,0:T(8,128)(2,1)}, u32[]{:S(2)}) copy-start(bf16[512,256]{1,0:T(8,128)(2,1)} %param.6) | copy-start | bytes 786436

commit v6 on v5

--- a/solution.py
+++ b/solution.py
@@ -83,7 +83,7 @@
 C_PARTS, D_PARTS = 2, 2
 Z_PARTS = 2
 ZPARTS = [pl.ds(m * (ROWS // Z_PARTS), ROWS // Z_PARTS) for m in range(Z_PARTS)]
-AHEAD = 0.7
+AHEAD = 0.9
 DELAY = {"core": 1.0, "far": 3.7, "x": 2.2, "o": 2.2, "y": 2.8, "z": 2.8}
 
 

time: 124 us -> 125 us (level)
  no operation moved by 1% of the time
where the time goes in v6:
time: 125 us
  Pallas kernels  121 us (97%)
  other arithmetic  2.61 us (2%)
    pallas_call x1, Pallas kernels, on_device(): pl.pallas_call(kernel, name='soap_step', out_shape=(jax.ShapeDtypeStruct(...  121 us
    add x1, other arithmetic, new_moments(): beta_second * second + (1.0 - beta_second) * rotated * rotated  2.61 us

profile of v6, /device:TPU:1, one launch (start us, length us, event | category | flops | bytes accessed | tf_op | source)
XLA Modules:
  0.0 124.5 jit_solution(14365209794361757860)
XLA Ops:
  0.6 0.0 copy-start.1
  0.6 0.0 copy-start
  0.7 0.0 copy-start.2
  0.7 121.2 %soap_step.1 = (f32[512,256]{1,0:T(8,128)}, f32[512,256]{1,0:T(8,128)}) custom-call(bf16[512,256]{1,0:T(8,128)(2,1)} %grad.1, f32[512,256]{1,0:T(8,128)} %moment_first.1, f32[512,256]{1,0:T(8,128)} %moment_second.1, bf16[128,512]{1,0:T(8,128)(2,1)} %ql.1, bf16[256,1024]{1,0:T(8,128)(2,1)} %qr.1), custom_call_target="tpu_custom_call" | custom-call | flops 6442450944 | bytes 4194304 | tf_op jit(solution)/shard_map/soap_step/pallas_call | solution.py:690
  121.9 0.0 copy-done.1
  121.9 0.0 copy-done
  121.9 0.0 copy-done.2
  121.9 2.6 %fusion.3 = (f32[512,256]{1,0:T(8,128)}, f32[512,256]{1,0:T(8,128)}, bf16[512,256]{1,0:T(8,128)(2,1)}, bf16[512,256]{1,0:T(8,128)(2,1)}) fusion(f32[512,256]{1,0:T(8,128)} %get-tuple-element.7, f32[512,256]{1,0:T(8,128)S(1)} %copy-done.1, f32[512,256]{1,0:T(8,128)S(1)} %copy-done, f32[512,256]{1,0:T(8,128)} %get-tuple-element.6, bf16[512,256]{1,0:T(8,128)(2,1)S(1)} %copy-done.2), kind=kLoop, calls=%fused_computation.6 | loop fusion | flops 1835008 | bytes 3932160 | tf_op jit(solution)/shard_map/add | solution.py:93
Async XLA Ops:
  0.6 121.2 %copy-start.1 = (f32[512,256]{1,0:T(8,128)S(1)}, f32[512,256]{1,0:T(8,128)}, u32[]{:S(2)}) copy-start(f32[512,256]{1,0:T(8,128)} %moment_second.1) | copy-start | bytes 1572868
  0.6 121.2 %copy-start = (f32[512,256]{1,0:T(8,128)S(1)}, f32[512,256]{1,0:T(8,128)}, u32[]{:S(2)}) copy-start(f32[512,256]{1,0:T(8,128)} %moment_first.1) | copy-start | bytes 1572868
  0.7 121.2 %copy-start.2 = (bf16[512,256]{1,0:T(8,128)(2,1)S(1)}, bf16[512,256]{1,0:T(8,128)(2,1)}, u32[]{:S(2)}) copy-start(bf16[512,256]{1,0:T(8,128)(2,1)} %param.6) | copy-start | bytes 786436
